TPU v7x, 32 devices: a whole 2x2x4 slice. The times are simulated.
32 devices in a mesh: slab: 2 (over y), ma: 4 (over z), freq: 2 (over x), pol: 2 (over core).
Axes of the slice: x: 2, y: 2, z: 4, core: 2. Of those that a mesh axis runs over, the one named last changes fastest.
Arguments:
- visibility: bfloat16 [16, 2, 64, 8192], P(('slab', 'freq'), None, 'pol', 'ma'), parts along dimension 0, may hold values from -6 to 6
- beam_rows: bfloat16 [16, 64, 768], P(('slab', 'freq'), 'pol'), parts along dimension 0, may hold values from -0.4375 to 0.4375
- mode_gain: float32 [192, 768], P('ma'), may hold values from 0.7 to 1.5
- harmonic_basis: bfloat16 [768, 768], replicated, may hold values from -0.21875 to 0.21875
- step_size: float32 [16], P(('slab', 'freq')), parts along dimension 0, may hold values from 0.15 to 0.25
- kl_matrix: bfloat16 [4, 8], P('slab'), parts along dimension 0, may hold values from -2 to 2
Outputs:
- filtered: bfloat16 [192, 4, 2, 768], P('ma', ('slab', 'freq'), 'pol'), parts along dimension 1
There are 2 independent parts, one for each index of `slab`. A program takes and returns all parts, laid end to end along the dimension named above; an argument that names none is the same for every part. Nothing has to cross between parts.
All inputs are finite; a program needn't handle non-finite values.
Results may differ from a plain program's by a relative error of at most 0.0088.
Values may be sent and summed in bfloat16 or wider, within the bound.
A program may use at most 64 MiB of HBM per device.

v0:
```python
import jax
import jax.numpy as jnp
from jax import lax
from jax.sharding import PartitionSpec as P

NT = 8192
ITERS = 2


def spectral_tables(time_index, mode_index, total):
    phase = time_index[:, None] * mode_index[None, :] % total
    angle = phase.astype(jnp.float32) * (2.0 * jnp.pi / total)
    return (jnp.cos(angle).astype(jnp.bfloat16), jnp.sin(angle).astype(jnp.bfloat16))


def transform_block(samples, cosine, sine):
    nfreq, nparts, nbase, ntime = samples.shape
    flat = samples.reshape(nfreq * nparts * nbase, ntime)
    width = cosine.shape[1]
    first = jnp.dot(flat, cosine, preferred_element_type=jnp.float32).reshape(
        nfreq, 2, nbase, width
    )
    second = jnp.dot(flat, sine, preferred_element_type=jnp.float32).reshape(nfreq, 2, nbase, width)
    return jnp.stack([first[:, 0] + second[:, 1], first[:, 1] - second[:, 0]], axis=1)


def on_device(visibility, beam_rows, mode_gain, harmonic_basis, step_size, kl_matrix):
    local_modes = mode_gain.shape[0]
    local_time = visibility.shape[3]
    degrees = harmonic_basis.shape[1]
    norm_scale = NT ** (-0.5)
    time_index = lax.axis_index("ma") * local_time + jnp.arange(local_time, dtype=jnp.int32)
    mode_index = jnp.arange(local_modes * lax.axis_size("ma"), dtype=jnp.int32)
    cosine, sine = spectral_tables(time_index, mode_index, NT)
    spectrum = lax.psum_scatter(
        transform_block(visibility, cosine, sine).transpose(3, 0, 1, 2),
        "ma",
        scatter_dimension=0,
        tiled=True,
    )
    modes = (spectrum * norm_scale).astype(jnp.bfloat16)
    mode_ids = lax.axis_index("ma") * local_modes + jnp.arange(local_modes, dtype=jnp.int32)
    mask = (jnp.arange(degrees, dtype=jnp.int32)[None, :] >= mode_ids[:, None]).astype(jnp.float32)
    gain = mode_gain[:, None, None, :]

    def back(signal, rows):
        total = jnp.einsum("mfpb,fbk->mfpk", signal, rows, preferred_element_type=jnp.float32)
        scaled = (total * gain).astype(jnp.bfloat16)
        result = jnp.dot(
            scaled.reshape(-1, degrees), harmonic_basis, preferred_element_type=jnp.float32
        )
        return result.reshape(scaled.shape) * mask[:, None, None, :]

    rows = lax.all_gather(beam_rows, "pol", axis=1, tiled=True)
    signal = lax.all_to_all(modes, "pol", split_axis=2, concat_axis=3, tiled=True)
    dirty = back(signal, rows)
    stepping = step_size[None, :, None, None]
    estimate = stepping * dirty
    for counter in range(ITERS):
        rounded = estimate.astype(jnp.bfloat16)
        sampled = jnp.einsum(
            "mfpl,kl->mfpk", rounded, harmonic_basis, preferred_element_type=jnp.float32
        )
        fore_scaled = (sampled * gain).astype(jnp.bfloat16)
        estimate = estimate + stepping * (
            dirty
            - back(
                jnp.einsum(
                    "mfpk,fbk->mfpb", fore_scaled, rows, preferred_element_type=jnp.float32
                ).astype(jnp.bfloat16),
                rows,
            )
        )
    rounded = estimate.astype(jnp.bfloat16)
    local_freqs = step_size.shape[0]
    columns = lax.dynamic_slice_in_dim(
        kl_matrix, lax.axis_index("freq") * local_freqs, local_freqs, 1
    )
    terms = jnp.einsum("jf,mfpl->mjpl", columns, rounded, preferred_element_type=jnp.float32)
    filtered = lax.psum_scatter(terms, "freq", scatter_dimension=1, tiled=True).astype(jnp.bfloat16)
    return filtered


def solution(mesh):
    placed = (
        P(("slab", "freq"), None, "pol", "ma"),
        P(("slab", "freq"), "pol", None),
        P("ma", None),
        P(),
        P(("slab", "freq")),
        P("slab", None),
    )
    return jax.shard_map(
        on_device,
        mesh=mesh,
        in_specs=placed,
        out_specs=P("ma", ("slab", "freq"), "pol", None),
        check_vma=False,
    )
```

profile of v0, /device:TPU:0, one launch (start us, length us, event | category | flops | bytes accessed | tf_op | source)
XLA Modules:
  0.0 77.3 jit_solution(14288232921664229300)
XLA Ops:
  6.5 0.0 copy-start
  6.5 0.0 reduce-scatter.7.cloned.1.call-start
  6.5 0.0 copy-start.5
  6.6 11.0 %convolution_bitcast_fusion.4 = f32[256,192]{0,1:T(8,128)S(1)} fusion(bf16[256,2048]{1,0:T(8,128)(2,1)} %bitcast.132, s32[2048]{0:T(1024)S(1)} %iota_add_fusion), kind=kOutput, calls=%fused_computation.45 | convolution fusion | flops 207224832 | bytes 1253376 | tf_op jit(solution)/shard_map/dot_general | solution.py:23
  17.5 0.0 copy-done.5
  17.5 7.9 %convolution_bitcast_fusion.5 = f32[256,192]{0,1:T(8,128)S(1)} fusion(bf16[256,2048]{1,0:T(8,128)(2,1)S(1)} %bitcast.133, s32[2048]{0:T(1024)S(1)} %iota_add_fusion), kind=kOutput, calls=%fused_computation.46 | convolution fusion | flops 207224832 | bytes 1253376 | tf_op jit(solution)/shard_map/dot_general | solution.py:20
  25.5 0.1 copy.16
  25.6 0.0 copy-start.2
  25.6 0.1 copy.15
  25.8 0.0 copy-start.1
  25.9 0.8 %copy.25 = f32[192,256]{1,0:T(8,128)} copy(f32[192,256]{0,1:T(8,128)S(1)} %bitcast.128) | data formatting | bytes 393216
  26.6 0.0 reduce-scatter.7.cloned.1.call-update
  26.7 0.0 reduce-scatter.5.cloned.1.call-start
  26.7 0.0 copy-done.2
  26.7 2.2 %all_gather.3 = bf16[4,64,768]{2,1,0:T(8,128)(2,1)S(1)} all-gather(bf16[4,32,768]{2,1,0:T(8,128)(2,1)S(1)} %copy-done.2), channel_id=1, replica_groups=mesh['slab'=2,'ma'=4,'freq'=2,'pol'=2] {'pol'}, dimensions={1}, use_global_device_ids=true | all-gather | bytes 589824 | tf_op jit(solution)/shard_map/all_gather | solution.py:54
  28.9 0.1 fusion.59
  29.0 19.9 %reduce-scatter.7.cloned.1.call-done = f32[48,256]{1,0:T(8,128)} async-done(((f32[192,256]{1,0:T(8,128)}), f32[48,256]{1,0:T(8,128)}) %reduce-scatter.7.cloned.1.call-update) | async-done | bytes 49168
  48.9 0.9 %copy.26 = f32[48,256]{0,1:T(8,128)S(1)} copy(f32[48,256]{1,0:T(8,128)} %reduce-scatter.7.cloned.1.call-done) | data formatting | bytes 98304
  49.8 0.1 reshape.118
  49.9 3.7 %all_to_all.4 = bf16[2,2,3072]{2,1,0:T(2,128)(2,1)S(1)} all-to-all(bf16[2,2,3072]{2,1,0:T(2,128)(2,1)S(1)} %reshape.118), channel_id=1, replica_groups=mesh['slab'=2,'ma'=4,'freq'=2,'pol'=2] {'pol'}, dimensions={0} | all-to-all | bytes 49152 | tf_op jit(solution)/shard_map/all_to_all | solution.py:55
  53.7 0.1 reshape.119
  53.8 0.0 copy-done
  53.8 0.0 copy-done.1
  53.8 0.0 copy-start.3
  53.8 0.6 convolution_multiply_fusion.4
  54.4 0.1 copy-done.3
  54.5 0.8 %fusion.44 = bf16[48,4,64]{2,0,1:T(8,128)(2,1)S(1)} fusion(bf16[4,64,768]{2,1,0:T(8,128)(2,1)S(1)} %all_gather.3, bf16[768,768]{1,0:T(8,128)(2,1)S(1)} %copy-done, f32[48,4,768]{2,0,1:T(8,128)S(1)} %convolution_multiply_fusion.4, f32[48,768]{1,0:T(8,128)S(1)} %copy-done.1, f32[4]{0:T(128)S(1)} %copy-done.3), kind=kOutput, calls=%fused_computation.50 | convolution fusion | flops 245968896 | bytes 2334736 | tf_op jit(solution)/shard_map/mfpk,fbk->mfpb/dot_general | solution.py:68
  55.3 0.5 fusion.8
  55.9 0.8 %fusion.41 = bf16[48,4,64]{2,0,1:T(8,128)(2,1)S(1)} fusion(bf16[4,64,768]{2,1,0:T(8,128)(2,1)S(1)} %all_gather.3, bf16[768,768]{1,0:T(8,128)(2,1)S(1)} %copy-done, f32[48,4,768]{2,0,1:T(8,128)S(1)} %fusion.8, f32[48,768]{1,0:T(8,128)S(1)} %copy-done.1), kind=kOutput, calls=%fused_computation.49 | convolution fusion | flops 245821440 | bytes 2334720 | tf_op jit(solution)/shard_map/mfpk,fbk->mfpb/dot_general | solution.py:68
  56.7 0.0 copy-start.4
  56.7 0.5 fusion.15
  57.3 0.1 copy-done.4
  57.4 0.4 convolution_bitcast_fusion.3
  57.8 0.7 copy.21
  58.5 0.0 reduce-scatter.5.cloned.1.call-update
  58.5 10.4 %reduce-scatter.5.cloned.1.call-done = f32[48,1,1,768]{3,0,2,1:T(8,128)} async-done(((f32[48,2,1,768]{3,0,2,1:T(8,128)}), f32[48,1,1,768]{3,0,2,1:T(8,128)}) %reduce-scatter.5.cloned.1.call-update) | async-done | bytes 147472 | tf_op jit(solution)/shard_map/reduce_scatter | solution.py:80
  68.9 1.6 %convert_element_type.96 = bf16[48,1,1,768]{3,0,2,1:T(8,128)(2,1)} convert(f32[48,1,1,768]{3,0,2,1:T(8,128)} %reduce-scatter.5.cloned.1.call-done) | non-fusion elementwise | flops 36864 | bytes 221184 | tf_op jit(solution)/shard_map/convert_element_type | solution.py:80
  (6 shorter events, 0.1 us)
Async XLA Ops:
  6.5 47.3 %copy-start = (bf16[768,768]{1,0:T(8,128)(2,1)S(1)}, bf16[768,768]{1,0:T(8,128)(2,1)}, u32[]{:S(2)}) copy-start(bf16[768,768]{1,0:T(8,128)(2,1)} %param.9) | copy-start | bytes 3538948
  6.5 42.3 %reduce-scatter.7.cloned.1.call-start = ((), (), s32[]{:S(2)}) async-start(), calls=%async_computation.4 | async-start | bytes 245760
  6.5 11.0 %copy-start.5 = (bf16[4,2,32,2048]{3,2,1,0:T(8,128)(2,1)S(1)}, bf16[4,2,32,2048]{3,2,1,0:T(8,128)(2,1)}, u32[]{:S(2)}) copy-start(bf16[4,2,32,2048]{3,2,1,0:T(8,128)(2,1)} %param.6) | copy-start | bytes 3145732
  25.6 1.1 %copy-start.2 = (bf16[4,32,768]{2,1,0:T(8,128)(2,1)S(1)}, bf16[4,32,768]{2,1,0:T(8,128)(2,1)}, u32[]{:S(2)}) copy-start(bf16[4,32,768]{2,1,0:T(8,128)(2,1)} %param.7) | copy-start | bytes 589828
  25.8 28.0 %copy-start.1 = (f32[48,768]{1,0:T(8,128)S(1)}, f32[48,768]{1,0:T(8,128)}, u32[]{:S(2)}) copy-start(f32[48,768]{1,0:T(8,128)} %param.8) | copy-start | bytes 442372
  26.7 42.2 %reduce-scatter.5.cloned.1.call-start = ((), (), s32[]{:S(2)}) async-start(), calls=%async_computation.3 | async-start | bytes 442368 | tf_op jit(solution)/shard_map/reduce_scatter | solution.py:80
  53.8 0.7 copy-start.3
  56.7 0.7 copy-start.4
Sparse Core Ops, SparseCore 0:
  26.8 22.0 reduce-scatter.6
  58.6 10.2 reduce-scatter.4
where the time goes:
time: 77.6 us; the launch traced here: 77.3 us
  waiting for transfers between devices  30.3 us (39%)
  matrix products  22.6 us (29%)
  between operations  13.6 us (18%)
  blocking collectives  5.91 us (8%)
  local copies, waits for them, and re-layouts  3.13 us (4%)
  other arithmetic  1.71 us (2%)
    unnamed x3, waiting for transfers between devices  19.9 us
    dot_general x1, matrix products, transform_block(): jnp.dot(flat, sine, preferred_element_type=jnp.float32)  11 us
    reduce_scatter x1, waiting for transfers between devices, on_device(): lax.psum_scatter(terms, 'freq', scatter_dimension=1, tiled=True)  10.4 us
    dot_general x1, matrix products, transform_block(): jnp.dot(flat, cosine, preferred_element_type=jnp.float32)  7.93 us
    all_to_all x1, blocking collectives, on_device(): lax.all_to_all(modes, 'pol', split_axis=2, concat_axis=3, tiled=True)  3.74 us
    all_gather x1, blocking collectives, on_device(): rows = lax.all_gather(beam_rows, 'pol', axis=1, tiled=True)  2.17 us
    unnamed x16, local copies, waits for them, and re-layouts  2.14 us
    dot_general x2, matrix products, on_device(): jnp.einsum('mfpk,fbk->mfpb', fore_scaled, rows, preferred_element_type=jn...  1.68 us
  transfers between devices with their start and end apart: 2, of which 2 were waited for; matrix products, arithmetic and copies ran while one was open for 0% of the time, Pallas kernels for 0%

commit v1 on v0

v1 whole, which is shorter than its diff:
```python
import functools

import jax
import jax.numpy as jnp
import ml_dtypes
import numpy as np
from jax import lax
from jax.experimental import pallas as pl
from jax.experimental.pallas import tpu as pltpu
from jax.sharding import PartitionSpec as P

ITERS = 2
MESH = pl.DeviceIdType.MESH
NT_DIMS = (((1,), (1,)), ((), ()))


def spectral_tables(modes, local_time, total):
    phase = np.outer(np.arange(modes), np.arange(local_time)) % total
    angle = phase * (2.0 * np.pi / total)
    both = np.concatenate([np.cos(angle), np.sin(angle)], axis=0)
    return both.astype(np.float32).astype(ml_dtypes.bfloat16)


def dot(left, right):
    return jnp.dot(left, right, preferred_element_type=jnp.float32)


def dot_t(left, right):
    return lax.dot_general(left, right, NT_DIMS, preferred_element_type=jnp.float32)


def kernel(
    sizes,
    vis_hbm,
    table_hbm,
    beam_hbm,
    gain_hbm,
    basis_hbm,
    step_ref,
    kl_ref,
    out_ref,
    vis_v,
    table_v,
    beam_v,
    gain_v,
    basis_v,
    dirty_v,
    est_v,
    send_v,
    recv_v,
    klsend_v,
    klrecv_v,
    load_sem,
    send_sem,
    recv_sem,
    beam_sem,
    klsend_sem,
    klrecv_sem,
):
    n_ma, n_pol, n_freq = sizes
    a, p, fr = lax.axis_index("ma"), lax.axis_index("pol"), lax.axis_index("freq")
    _, nfreq, nbase, ntime = vis_v.shape
    local_modes, degrees = gain_v.shape
    all_modes = local_modes * n_ma
    half = nfreq * nbase
    peers = [(da, dp) for da in range(n_ma) for dp in range(n_pol) if (da, dp) != (0, 0)]
    peers.sort(key=lambda o: (abs(o[0] - n_ma // 2), o[1]))

    tchunks = table_v.shape[0]
    tsize = ntime // tchunks
    spectral = []
    for i in range(tchunks):
        cols = pl.ds(i * tsize, tsize)
        group = [
            pltpu.make_async_copy(
                vis_hbm.at[:, part, :, cols], vis_v.at[part, :, :, cols], load_sem.at[3 * i + part]
            )
            for part in range(2)
        ]
        group.append(pltpu.make_async_copy(table_hbm.at[i], table_v.at[i], load_sem.at[3 * i + 2]))
        for c in group:
            c.start()
        spectral.append(group)
    base = 3 * tchunks
    load_beam = pltpu.make_async_copy(beam_hbm, beam_v.at[p], load_sem.at[base])
    load_gain = pltpu.make_async_copy(gain_hbm, gain_v, load_sem.at[base + 1])
    load_basis = pltpu.make_async_copy(basis_hbm, basis_v, load_sem.at[base + 2])
    for c in (load_beam, load_gain, load_basis):
        c.start()

    barrier = pltpu.get_barrier_semaphore()

    def group_id(da, dp):
        return {"ma": lax.rem(a + da, n_ma), "pol": lax.rem(p + dp, n_pol)}

    def freq_id(df):
        return {"freq": lax.rem(fr + df, n_freq)}

    for da, dp in peers:
        pl.semaphore_signal(barrier, inc=1, device_id=group_id(da, dp), device_id_type=MESH)
    for df in range(1, n_freq):
        pl.semaphore_signal(barrier, inc=1, device_id=freq_id(df), device_id_type=MESH)

    total = None
    for i in range(tchunks):
        for c in spectral[i]:
            c.wait()
        samples = vis_v[:, :, :, i * tsize : (i + 1) * tsize].reshape(2 * half, tsize)
        term = dot_t(table_v[i], samples)
        total = term if total is None else total + term
    cosine, sine = total[:all_modes], total[all_modes:]
    real = cosine[:, :half] + sine[:, half:]
    imag = cosine[:, half:] - sine[:, :half]
    turn = lax.rem(a * lax.broadcasted_iota(jnp.int32, (all_modes, half), 0), n_ma)
    scale = float(ntime * n_ma) ** -0.5
    pc = jnp.full((all_modes, half), scale, jnp.float32)
    ps = jnp.zeros((all_modes, half), jnp.float32)
    for r in range(1, n_ma):
        angle = 2.0 * np.pi * r / n_ma
        pc = jnp.where(turn == r, float(scale * np.cos(angle)), pc)
        ps = jnp.where(turn == r, float(scale * np.sin(angle)), ps)
    block = (n_ma, local_modes, half)
    send_v[0] = (real * pc + imag * ps).astype(jnp.bfloat16).reshape(block)
    send_v[1] = (imag * pc - real * ps).astype(jnp.bfloat16).reshape(block)

    pl.semaphore_wait(barrier, len(peers) + n_freq - 1)
    copies = []
    for i, (da, dp) in enumerate(peers):
        to = group_id(da, dp)
        copy = pltpu.make_async_remote_copy(
            src_ref=send_v.at[to["pol"], to["ma"]],
            dst_ref=recv_v.at[p, a],
            send_sem=send_sem.at[i],
            recv_sem=recv_sem.at[i],
            device_id=to,
            device_id_type=MESH,
        )
        copy.start()
        copies.append(copy)
    beam_copies = []
    for dp in range(1, n_pol):
        copy = pltpu.make_async_remote_copy(
            src_ref=beam_hbm,
            dst_ref=beam_v.at[p],
            send_sem=beam_sem.at[0, dp - 1],
            recv_sem=beam_sem.at[1, dp - 1],
            device_id={"pol": lax.rem(p + dp, n_pol)},
            device_id_type=MESH,
        )
        copy.start()
        beam_copies.append(copy)
    recv_v[p, a] = send_v[p, a]

    kl = kl_ref[...].astype(jnp.float32)
    kl_row = lax.broadcasted_iota(jnp.int32, kl.shape, 0)
    kl_col = lax.broadcasted_iota(jnp.int32, kl.shape, 1)
    kept = kl.shape[0] // n_freq
    weights = []
    for df in range(n_freq):
        first = lax.rem(fr + df, n_freq) * kept
        weights.append(
            [
                [
                    jnp.sum(
                        jnp.where((kl_row == first + j) & (kl_col == fr * nfreq + f), kl, 0.0),
                        axis=(0, 1),
                        keepdims=True,
                    )
                    for f in range(nfreq)
                ]
                for j in range(kept)
            ]
        )
    for c in (load_beam, load_gain, load_basis):
        c.wait()
    lane = lax.rem(lax.broadcasted_iota(jnp.int32, (local_modes, n_pol * half), 1), half)
    own = [(lane >= f * nbase) & (lane < (f + 1) * nbase) for f in range(nfreq)]
    mode = lax.broadcasted_iota(jnp.int32, (local_modes, degrees), 0) + a * local_modes
    keep = lax.broadcasted_iota(jnp.int32, (local_modes, degrees), 1) >= mode

    for copy in beam_copies:
        copy.wait_recv()
    for copy in copies:
        copy.wait_recv()

    def spread(blocks):
        return jnp.concatenate(
            [jnp.where(own[f], blocks[f], 0.0) for f in range(nfreq)], axis=0
        ).astype(jnp.bfloat16)

    def with_gain(value):
        value = value.reshape(nfreq, local_modes, degrees) * gain_v[...][None]
        return value.astype(jnp.bfloat16).reshape(nfreq * local_modes, degrees)

    def rows():
        return beam_v[...].reshape(n_pol * half, degrees)

    def fore(x):
        q = with_gain(dot_t(x, basis_v[...]))
        y = dot_t(q, rows())
        return spread([y[f * local_modes : (f + 1) * local_modes] for f in range(nfreq)])

    halves = []
    for q in range(n_pol):
        summed = recv_v[q, 0].astype(jnp.float32)
        for s in range(1, n_ma):
            summed = summed + recv_v[q, s].astype(jnp.float32)
        halves.append(summed)
    signal = spread([jnp.concatenate(halves, axis=1)] * nfreq)

    dirty = dot(with_gain(dot(signal, rows())), basis_v[...])
    for f in range(nfreq):
        value = jnp.where(keep, dirty[f * local_modes : (f + 1) * local_modes], 0.0)
        dirty_v[f] = value
        est_v[f] = value * step_ref[f]

    def rounded():
        return est_v[...].astype(jnp.bfloat16).reshape(nfreq * local_modes, degrees)

    for _ in range(ITERS - 1):
        again = dot(with_gain(dot(fore(rounded()), rows())), basis_v[...])
        for f in range(nfreq):
            value = jnp.where(keep, again[f * local_modes : (f + 1) * local_modes], 0.0)
            est_v[f] = est_v[f] + step_ref[f] * (dirty_v[f] - value)

    h = with_gain(dot(fore(rounded()), rows()))
    chunks = klsend_v.shape[1]
    width = degrees // chunks
    kl_copies = []
    held = []
    for i in range(chunks):
        cols = slice(i * width, (i + 1) * width)
        again = dot(h, basis_v[:, cols])
        final = []
        for f in range(nfreq):
            value = jnp.where(keep[:, cols], again[f * local_modes : (f + 1) * local_modes], 0.0)
            value = est_v[f, :, cols] + step_ref[f] * (dirty_v[f, :, cols] - value)
            final.append(value.astype(jnp.bfloat16).astype(jnp.float32))
        group = []
        for df in [*range(1, n_freq), 0]:
            terms = []
            for j in range(kept):
                term = weights[df][j][0] * final[0]
                for f in range(1, nfreq):
                    term = term + weights[df][j][f] * final[f]
                terms.append(term)
            if df == 0:
                held.append(terms)
                continue
            for j in range(kept):
                klsend_v[df - 1, i, j] = terms[j].astype(jnp.bfloat16)
            copy = pltpu.make_async_remote_copy(
                src_ref=klsend_v.at[df - 1, i],
                dst_ref=klrecv_v.at[df - 1, i],
                send_sem=klsend_sem.at[df - 1, i],
                recv_sem=klrecv_sem.at[df - 1, i],
                device_id=freq_id(df),
                device_id_type=MESH,
            )
            copy.start()
            group.append(copy)
        kl_copies.append(group)

    for copy in copies:
        copy.wait_send()
    for copy in beam_copies:
        copy.wait_send()
    for i in range(chunks):
        for df, copy in enumerate(kl_copies[i], 1):
            copy.wait_recv()
            for j in range(kept):
                held[i][j] = held[i][j] + klrecv_v[df - 1, i, j].astype(jnp.float32)
        for j in range(kept):
            out_ref[j, :, i * width : (i + 1) * width] = held[i][j].astype(jnp.bfloat16)
    for group in kl_copies:
        for copy in group:
            copy.wait_send()


def on_device(sizes, visibility, beam_rows, mode_gain, harmonic_basis, step_size, kl_matrix):
    n_ma, n_pol, n_freq = sizes
    nfreq, _, nbase, ntime = visibility.shape
    local_modes, degrees = mode_gain.shape
    kept = kl_matrix.shape[0] // n_freq
    half = nfreq * nbase
    all_modes = local_modes * n_ma
    tchunks = 2 if ntime % 512 == 0 else 1
    chunks = 3 if degrees % 384 == 0 else 1
    table = spectral_tables(all_modes, ntime, ntime * n_ma)
    table = np.ascontiguousarray(table.reshape(2 * all_modes, tchunks, -1).transpose(1, 0, 2))
    peers = n_ma * n_pol - 1
    hops = max(n_freq - 1, 1)
    dma = pltpu.SemaphoreType.DMA
    kl_shape = (hops, chunks, kept, local_modes, degrees // chunks)
    out = pl.pallas_call(
        functools.partial(kernel, sizes),
        out_shape=jax.ShapeDtypeStruct((kept, local_modes, degrees), jnp.bfloat16),
        in_specs=[pl.BlockSpec(memory_space=pl.ANY)] * 5
        + [pl.BlockSpec(memory_space=pltpu.SMEM), pl.BlockSpec(memory_space=pltpu.VMEM)],
        out_specs=pl.BlockSpec(memory_space=pltpu.VMEM),
        scratch_shapes=[
            pltpu.VMEM((2, nfreq, nbase, ntime), jnp.bfloat16),
            pltpu.VMEM(table.shape, jnp.bfloat16),
            pltpu.VMEM((n_pol, nfreq, nbase, degrees), jnp.bfloat16),
            pltpu.VMEM((local_modes, degrees), jnp.float32),
            pltpu.VMEM(harmonic_basis.shape, jnp.bfloat16),
            pltpu.VMEM((nfreq, local_modes, degrees), jnp.float32),
            pltpu.VMEM((nfreq, local_modes, degrees), jnp.float32),
            pltpu.VMEM((2, n_ma, local_modes, half), jnp.bfloat16),
            pltpu.VMEM((n_pol, n_ma, local_modes, half), jnp.bfloat16),
            pltpu.VMEM(kl_shape, jnp.bfloat16),
            pltpu.VMEM(kl_shape, jnp.bfloat16),
            dma((3 * tchunks + 3,)),
            dma((peers,)),
            dma((peers,)),
            dma((2, max(n_pol - 1, 1))),
            dma((hops, chunks)),
            dma((hops, chunks)),
        ],
        compiler_params=pltpu.CompilerParams(
            collective_id=0, has_side_effects=True, vmem_limit_bytes=56 * 2**20
        ),
    )(
        visibility,
        jnp.asarray(table),
        beam_rows,
        mode_gain,
        harmonic_basis,
        step_size,
        kl_matrix,
    )
    return out.transpose(1, 0, 2)[:, :, None, :]


def solution(mesh):
    sizes = (mesh.shape["ma"], mesh.shape["pol"], mesh.shape["freq"])
    placed = (
        P(("slab", "freq"), None, "pol", "ma"),
        P(("slab", "freq"), "pol", None),
        P("ma", None),
        P(),
        P(("slab", "freq")),
        P("slab", None),
    )
    return jax.shard_map(
        functools.partial(on_device, sizes),
        mesh=mesh,
        in_specs=placed,
        out_specs=P("ma", ("slab", "freq"), "pol", None),
        check_vma=False,
    )
```

time: 77.6 us -> 19.9 us (0.26)
  waiting for transfers between devices: 30.3 us -> 0 us
  matrix products: 22.6 us -> 0 us
  Pallas kernels: 0 us -> 18.2 us
  between operations: 13.6 us -> 0.01 us
  blocking collectives: 5.91 us -> 0 us
  other arithmetic: 1.71 us -> 0 us
  local copies, waits for them, and re-layouts: 3.13 us -> 1.52 us
    dot_general x8 -> x0, matrix products: 22.6 us -> none  [the longest x1 11 us: transform_block(): jnp.dot(flat, sine, preferred_element_type=jnp.float32)]
    unnamed x3 -> x0, waiting for transfers between devices: 19.9 us -> none
    pallas_call x0 -> x1, Pallas kernels: none -> 18.2 us  [on_device(): pl.pallas_call(functools.partial(kernel, sizes), out_shape=jax.ShapeDtype...]
    reduce_scatter x1 -> x0, waiting for transfers between devices: 10.4 us -> none  [on_device(): lax.psum_scatter(terms, 'freq', scatter_dimension=1, tiled=True)]
    all_to_all x1 -> x0, blocking collectives: 3.74 us -> none  [on_device(): lax.all_to_all(modes, 'pol', split_axis=2, concat_axis=3, tiled=True)]
    all_gather x1 -> x0, blocking collectives: 2.17 us -> none  [on_device(): rows = lax.all_gather(beam_rows, 'pol', axis=1, tiled=True)]
    convert_element_type x2 -> x0, other arithmetic: 1.63 us -> none  [the longest x1 1.55 us: on_device(): lax.psum_scatter(terms, 'freq', scatter_dimension=1, tiled=True)]
    unnamed x16 -> x1, local copies, waits for them, and re-layouts: 2.14 us -> 1.52 us
  transfers between devices with their start and end apart: 2 -> 0, of which waited for: 2 -> 0; matrix products, arithmetic and copies ran while one was open for 0% -> 0% of each run, Pallas kernels for 0% -> 0%
where the time goes in v1:
time: 19.9 us; the launch traced here: 19.7 us
  Pallas kernels  18.2 us (91%)
  local copies, waits for them, and re-layouts  1.52 us (8%)
    pallas_call x1, Pallas kernels, on_device(): pl.pallas_call(functools.partial(kernel, sizes), out_shape=jax.ShapeDtype...  18.2 us
    unnamed x1, local copies, waits for them, and re-layouts  1.52 us

profile of v1, /device:TPU:0, one launch (start us, length us, event | category | flops | bytes accessed | tf_op | source)
XLA Modules:
  0.0 19.7 jit_solution(11583498152388559798)
XLA Ops:
  0.0 18.2 %shard_map.73 = bf16[1,48,768]{2,1,0:T(8,128)(2,1)} custom-call(bf16[4,2,32,2048]{3,2,1,0:T(8,128)(2,1)} %vis_hbm.1, bf16[2,384,1024]{2,1,0:T(8,128)(2,1)} %constant.2.clone.table_hbm, bf16[4,32,768]{2,1,0:T(8,128)(2,1)} %beam_hbm.1, f32[48,768]{1,0:T(8,128)} %gain_hbm.1, bf16[768,768]{1,0:T(8,128)(2,1)} %basis_hbm.1, f32[4]{0:T(128)} %step_ref.1, ...), custom_call_target="tpu_custom_call" | custom-call | tf_op jit(solution)/shard_map/pallas_call | solution.py:295
  18.2 1.5 %copy.9 = bf16[48,1,1,768]{3,0,2,1:T(8,128)(2,1)} copy(bf16[48,1,1,768]{3,0,2,1:T(8,128)(2,1)} %bitcast.1) | data formatting | bytes 147456

commit v2 on v1

v2 whole, which is shorter than its diff:
```python
import functools

import jax
import jax.numpy as jnp
import ml_dtypes
import numpy as np
from jax import lax
from jax.experimental import pallas as pl
from jax.experimental.pallas import tpu as pltpu
from jax.sharding import PartitionSpec as P

ITERS = 2
MESH = pl.DeviceIdType.MESH
NT_DIMS = (((1,), (1,)), ((), ()))


def spectral_tables(modes, local_time, total):
    phase = np.outer(np.arange(modes), np.arange(local_time)) % total
    angle = phase * (2.0 * np.pi / total)
    both = np.concatenate([np.cos(angle), np.sin(angle)], axis=0)
    return both.astype(np.float32).astype(ml_dtypes.bfloat16)


def dot(left, right):
    return jnp.dot(left, right, preferred_element_type=jnp.float32)


def dot_t(left, right):
    return lax.dot_general(left, right, NT_DIMS, preferred_element_type=jnp.float32)


def kernel(
    sizes,
    vis_hbm,
    table_hbm,
    beam_hbm,
    gain_hbm,
    basis_hbm,
    step_hbm,
    kl_hbm,
    out_ref,
    vis_v,
    table_v,
    beam_v,
    gain_v,
    basis_v,
    step_s,
    kl_v,
    send_v,
    recv_v,
    ysend_v,
    yrecv_v,
    load_sem,
    send_sem,
    recv_sem,
    pol_sem,
    freq_sem,
    pass_sem,
    y_sem,
):
    n_ma, n_pol, n_freq = sizes
    a, p, fr = lax.axis_index("ma"), lax.axis_index("pol"), lax.axis_index("freq")
    _, nfreq, nbase, ntime = vis_v.shape
    local_modes, degrees = gain_v.shape
    all_modes = local_modes * n_ma
    half = nfreq * nbase
    full = n_pol * half
    kept = kl_v.shape[0] // n_freq
    peers = [(da, dp) for da in range(n_ma) for dp in range(n_pol) if (da, dp) != (0, 0)]
    peers.sort(key=lambda o: (abs(o[0] - n_ma // 2), o[1]))

    tchunks = table_v.shape[0]
    tsize = ntime // tchunks
    spectral = []
    for i in range(tchunks):
        cols = pl.ds(i * tsize, tsize)
        group = [
            pltpu.make_async_copy(
                vis_hbm.at[:, part, :, cols], vis_v.at[part, :, :, cols], load_sem.at[3 * i + part]
            )
            for part in range(2)
        ]
        group.append(pltpu.make_async_copy(table_hbm.at[i], table_v.at[i], load_sem.at[3 * i + 2]))
        for c in group:
            c.start()
        spectral.append(group)
    loads = [
        pltpu.make_async_copy(src, dst, load_sem.at[3 * tchunks + i])
        for i, (src, dst) in enumerate(
            [
                (step_hbm, step_s),
                (kl_hbm, kl_v),
                (basis_hbm, basis_v),
                (beam_hbm, beam_v.at[fr, p]),
                (gain_hbm, gain_v),
            ]
        )
    ]
    for c in loads:
        c.start()

    barrier = pltpu.get_barrier_semaphore()

    def group_id(da, dp):
        return {"ma": lax.rem(a + da, n_ma), "pol": lax.rem(p + dp, n_pol)}

    def freq_id(df):
        return {"freq": lax.rem(fr + df, n_freq)}

    def remote(src, dst, send, recv, to):
        copy = pltpu.make_async_remote_copy(
            src_ref=src,
            dst_ref=dst,
            send_sem=send,
            recv_sem=recv,
            device_id=to,
            device_id_type=MESH,
        )
        copy.start()
        return copy

    for da, dp in peers:
        pl.semaphore_signal(barrier, inc=1, device_id=group_id(da, dp), device_id_type=MESH)
    for df in range(1, n_freq):
        pl.semaphore_signal(barrier, inc=1, device_id=freq_id(df), device_id_type=MESH)

    total = None
    for i in range(tchunks):
        for c in spectral[i]:
            c.wait()
        samples = vis_v[:, :, :, i * tsize : (i + 1) * tsize].reshape(2 * half, tsize)
        term = dot_t(table_v[i], samples)
        total = term if total is None else total + term
    cosine, sine = total[:all_modes], total[all_modes:]
    real = cosine[:, :half] + sine[:, half:]
    imag = cosine[:, half:] - sine[:, :half]
    turn = lax.rem(a * lax.broadcasted_iota(jnp.int32, (all_modes, half), 0), n_ma)
    scale = float(ntime * n_ma) ** -0.5
    pc = jnp.full((all_modes, half), scale, jnp.float32)
    ps = jnp.zeros((all_modes, half), jnp.float32)
    for r in range(1, n_ma):
        angle = 2.0 * np.pi * r / n_ma
        pc = jnp.where(turn == r, float(scale * np.cos(angle)), pc)
        ps = jnp.where(turn == r, float(scale * np.sin(angle)), ps)
    block = (n_ma, local_modes, half)
    send_v[0] = (real * pc + imag * ps).astype(jnp.bfloat16).reshape(block)
    send_v[1] = (imag * pc - real * ps).astype(jnp.bfloat16).reshape(block)

    pl.semaphore_wait(barrier, len(peers) + n_freq - 1)
    copies = []
    for i, (da, dp) in enumerate(peers):
        to = group_id(da, dp)
        src = send_v.at[to["pol"], to["ma"]]
        copies.append(remote(src, recv_v.at[p, a], send_sem.at[i], recv_sem.at[i], to))
    mine = beam_v.at[fr, p]
    pol_copies = [
        remote(beam_hbm, mine, pol_sem.at[0, d - 1], pol_sem.at[1, d - 1], group_id(0, d))
        for d in range(1, n_pol)
    ]
    freq_copies = [
        remote(beam_hbm, mine, freq_sem.at[0, d - 1], freq_sem.at[1, d - 1], freq_id(d))
        for d in range(1, n_freq)
    ]
    recv_v[p, a] = send_v[p, a]

    for c in loads:
        c.wait()
    lane = lax.rem(lax.broadcasted_iota(jnp.int32, (local_modes, full), 1), half)
    own = [(lane >= f * nbase) & (lane < (f + 1) * nbase) for f in range(nfreq)]
    mode = lax.broadcasted_iota(jnp.int32, (local_modes, degrees), 0) + a * local_modes
    keep = lax.broadcasted_iota(jnp.int32, (local_modes, degrees), 1) >= mode
    kl = kl_v[...].astype(jnp.float32)
    kl_row = lax.broadcasted_iota(jnp.int32, kl.shape, 0)
    kl_col = lax.broadcasted_iota(jnp.int32, kl.shape, 1)

    def kl_weight(j, f):
        chosen = (kl_row == j) & (kl_col == fr * nfreq + f)
        return jnp.sum(jnp.where(chosen, kl, 0.0), axis=(0, 1), keepdims=True)

    def lane_weights(df):
        weights = []
        for j in range(kept):
            row = jnp.zeros((1, full), jnp.float32)
            for f in range(nfreq):
                value = kl_weight(lax.rem(fr + df, n_freq) * kept + j, f)
                row = jnp.where(own[f][:1], value, row)
            weights.append(row)
        return weights

    weights = [lane_weights(df) for df in range(n_freq)]
    steps = jnp.zeros((1, full), jnp.float32)
    for f in range(nfreq):
        steps = jnp.where(own[f][:1], step_s[f], steps)

    for copy in pol_copies + copies:
        copy.wait_recv()

    def spread(value):
        return jnp.concatenate(
            [jnp.where(own[f], value, 0.0) for f in range(nfreq)], axis=0
        ).astype(jnp.bfloat16)

    def gather(value):
        result = jnp.zeros((local_modes, full), jnp.float32)
        for f in range(nfreq):
            result = jnp.where(own[f], value[f * local_modes : (f + 1) * local_modes], result)
        return result

    def with_gain(value):
        value = value.reshape(-1, local_modes, degrees) * gain_v[...][None]
        return value.astype(jnp.bfloat16).reshape(-1, degrees)

    def masked(value):
        value = value.reshape(-1, local_modes, degrees)
        return jnp.where(keep[None], value, 0.0).astype(jnp.bfloat16).reshape(-1, degrees)

    def again(y):
        rows = beam_v[fr].reshape(full, degrees)
        coeffs = masked(dot(with_gain(dot(spread(y), rows)), basis_v[...]))
        return gather(dot_t(with_gain(dot_t(coeffs, basis_v[...])), rows))

    halves = []
    for q in range(n_pol):
        summed = recv_v[q, 0].astype(jnp.float32)
        for s in range(1, n_ma):
            summed = summed + recv_v[q, s].astype(jnp.float32)
        halves.append(summed)
    z = steps * jnp.concatenate(halves, axis=1)
    y = z
    pass_copies = []
    for it in range(ITERS):
        y = y + z - steps * again(y)
        if it == 0:
            for d, copy in enumerate(freq_copies, 1):
                copy.wait_recv()
                slot = beam_v.at[lax.rem(fr + n_freq - d, n_freq), p]
                for dp in range(1, n_pol):
                    sems = (pass_sem.at[0, d - 1, dp - 1], pass_sem.at[1, d - 1, dp - 1])
                    pass_copies.append(remote(slot, slot, *sems, group_id(0, dp)))

    y_copies = []
    for d in range(1, n_freq):
        for j in range(kept):
            ysend_v[d - 1, j] = (y * weights[d][j]).astype(jnp.bfloat16)
        sems = (y_sem.at[0, d - 1], y_sem.at[1, d - 1])
        y_copies.append(remote(ysend_v.at[d - 1], yrecv_v.at[fr], *sems, freq_id(d)))
    for j in range(kept):
        yrecv_v[fr, j] = (y * weights[0][j]).astype(jnp.bfloat16)

    for copy in pass_copies + y_copies:
        copy.wait_recv()
    left = jnp.concatenate(
        [yrecv_v[s].reshape(kept * local_modes, full) for s in range(n_freq)], axis=1
    )
    g = dot(left, beam_v[...].reshape(n_freq * full, degrees))
    out_ref[...] = masked(dot(with_gain(g), basis_v[...])).reshape(out_ref.shape)
    for copy in copies + pol_copies + freq_copies + pass_copies + y_copies:
        copy.wait_send()


def store_kernel(src, dst, sem):
    copy = pltpu.make_async_copy(src, dst, sem)
    copy.start()
    copy.wait()


def on_device(sizes, visibility, beam_rows, mode_gain, harmonic_basis, step_size, kl_matrix):
    n_ma, n_pol, n_freq = sizes
    nfreq, _, nbase, ntime = visibility.shape
    local_modes, degrees = mode_gain.shape
    kept = kl_matrix.shape[0] // n_freq
    half = nfreq * nbase
    full = n_pol * half
    all_modes = local_modes * n_ma
    tchunks = 2 if ntime % 512 == 0 else 1
    table = spectral_tables(all_modes, ntime, ntime * n_ma)
    table = np.ascontiguousarray(table.reshape(2 * all_modes, tchunks, -1).transpose(1, 0, 2))
    peers = n_ma * n_pol - 1
    hops, cores = max(n_freq - 1, 1), max(n_pol - 1, 1)
    dma = pltpu.SemaphoreType.DMA
    out_shape = (kept, local_modes, degrees)
    out = pl.pallas_call(
        functools.partial(kernel, sizes),
        out_shape=pltpu.VMEM(out_shape, jnp.bfloat16),
        in_specs=[pl.BlockSpec(memory_space=pl.ANY)] * 7,
        out_specs=pl.BlockSpec(memory_space=pltpu.VMEM),
        scratch_shapes=[
            pltpu.VMEM((2, nfreq, nbase, ntime), jnp.bfloat16),
            pltpu.VMEM(table.shape, jnp.bfloat16),
            pltpu.VMEM((n_freq, n_pol, nfreq, nbase, degrees), jnp.bfloat16),
            pltpu.VMEM((local_modes, degrees), jnp.float32),
            pltpu.VMEM(harmonic_basis.shape, jnp.bfloat16),
            pltpu.SMEM(step_size.shape, jnp.float32),
            pltpu.VMEM(kl_matrix.shape, jnp.bfloat16),
            pltpu.VMEM((2, n_ma, local_modes, half), jnp.bfloat16),
            pltpu.VMEM((n_pol, n_ma, local_modes, half), jnp.bfloat16),
            pltpu.VMEM((hops, kept, local_modes, full), jnp.bfloat16),
            pltpu.VMEM((n_freq, kept, local_modes, full), jnp.bfloat16),
            dma((3 * tchunks + 5,)),
            dma((peers,)),
            dma((peers,)),
            dma((2, cores)),
            dma((2, hops)),
            dma((2, hops, cores)),
            dma((2, hops)),
        ],
        compiler_params=pltpu.CompilerParams(
            collective_id=0, has_side_effects=True, vmem_limit_bytes=56 * 2**20
        ),
    )(
        visibility,
        jnp.asarray(table),
        beam_rows,
        mode_gain,
        harmonic_basis,
        step_size,
        kl_matrix,
    )
    out = pl.pallas_call(
        store_kernel,
        out_shape=jax.ShapeDtypeStruct(out_shape, jnp.bfloat16),
        in_specs=[pl.BlockSpec(memory_space=pl.ANY)],
        out_specs=pl.BlockSpec(memory_space=pl.ANY),
        scratch_shapes=[dma],
    )(out)
    return out.transpose(1, 0, 2)[:, :, None, :]


def solution(mesh):
    sizes = (mesh.shape["ma"], mesh.shape["pol"], mesh.shape["freq"])
    placed = (
        P(("slab", "freq"), None, "pol", "ma"),
        P(("slab", "freq"), "pol", None),
        P("ma", None),
        P(),
        P(("slab", "freq")),
        P("slab", None),
    )
    return jax.shard_map(
        functools.partial(on_device, sizes),
        mesh=mesh,
        in_specs=placed,
        out_specs=P("ma", ("slab", "freq"), "pol", None),
        check_vma=False,
    )
```

time: 19.9 us -> 20.5 us (1.030)
  Pallas kernels: 18.2 us -> 19.7 us
  local copies, waits for them, and re-layouts: 1.52 us -> 0.61 us
    pallas_call x1 -> x2, Pallas kernels: 18.2 us -> 19.7 us  [the longest x1 16.4 us: on_device(): pl.pallas_call(functools.partial(kernel, sizes), out_shape=pltpu.VMEM(out...]
    unnamed x1 -> x2, local copies, waits for them, and re-layouts: 1.52 us -> 0.61 us
where the time goes in v2:
time: 20.5 us; the launch traced here: 20.4 us
  Pallas kernels  19.7 us (96%)
  local copies, waits for them, and re-layouts  0.61 us (3%)
    pallas_call x1, Pallas kernels, on_device(): pl.pallas_call(functools.partial(kernel, sizes), out_shape=pltpu.VMEM(out...  16.4 us
    pallas_call x1, Pallas kernels, on_device(): pl.pallas_call(store_kernel, out_shape=jax.ShapeDtypeStruct(out_shape, jn...  3.34 us
    unnamed x2, local copies, waits for them, and re-layouts  0.61 us

profile of v2, /device:TPU:0, one launch (start us, length us, event | category | flops | bytes accessed | tf_op | source)
XLA Modules:
  0.0 20.4 jit_solution(9210067793895173009)
XLA Ops:
  0.0 16.4 %shard_map.73.src = bf16[1,48,768]{2,1,0:T(8,128)(2,1)S(1)} custom-call(bf16[4,2,32,2048]{3,2,1,0:T(8,128)(2,1)} %vis_hbm.1, bf16[2,384,1024]{2,1,0:T(8,128)(2,1)} %constant.2.clone.table_hbm, bf16[4,32,768]{2,1,0:T(8,128)(2,1)} %beam_hbm.1, f32[48,768]{1,0:T(8,128)} %gain_hbm.1, bf16[768,768]{1,0:T(8,128)(2,1)} %basis_hbm.1, f32[4]{0:T(128)} %step_hbm.1, ...), custom_call_target="tpu_custom_call" | custom-call | tf_op jit(solution)/shard_map/pallas_call | solution.py:282
  16.4 0.0 copy-start
  16.4 0.6 %copy-done = bf16[1,48,768]{2,1,0:T(8,128)(2,1)} copy-done((bf16[1,48,768]{2,1,0:T(8,128)(2,1)}, bf16[1,48,768]{2,1,0:T(8,128)(2,1)S(1)}, u32[]{:S(2)}) %copy-start) | copy-done | bytes 73752
  17.0 3.3 %shard_map.74 = bf16[1,48,768]{2,1,0:T(8,128)(2,1)} custom-call(bf16[1,48,768]{2,1,0:T(8,128)(2,1)} %copy-done), custom_call_target="tpu_custom_call" | custom-call | tf_op jit(solution)/shard_map/pallas_call | solution.py:319
Async XLA Ops:
  16.4 0.6 %copy-start = (bf16[1,48,768]{2,1,0:T(8,128)(2,1)}, bf16[1,48,768]{2,1,0:T(8,128)(2,1)S(1)}, u32[]{:S(2)}) copy-start(bf16[1,48,768]{2,1,0:T(8,128)(2,1)S(1)} %shard_map.73.src) | copy-start | bytes 221188

commit v3 on v2

--- a/solution.py
+++ b/solution.py
@@ -256,12 +256,6 @@
     out_ref[...] = masked(dot(with_gain(g), basis_v[...])).reshape(out_ref.shape)
     for copy in copies + pol_copies + freq_copies + pass_copies + y_copies:
         copy.wait_send()
-
-
-def store_kernel(src, dst, sem):
-    copy = pltpu.make_async_copy(src, dst, sem)
-    copy.start()
-    copy.wait()
 
 
 def on_device(sizes, visibility, beam_rows, mode_gain, harmonic_basis, step_size, kl_matrix):
@@ -316,13 +310,6 @@
         step_size,
         kl_matrix,
     )
-    out = pl.pallas_call(
-        store_kernel,
-        out_shape=jax.ShapeDtypeStruct(out_shape, jnp.bfloat16),
-        in_specs=[pl.BlockSpec(memory_space=pl.ANY)],
-        out_specs=pl.BlockSpec(memory_space=pl.ANY),
-        scratch_shapes=[dma],
-    )(out)
     return out.transpose(1, 0, 2)[:, :, None, :]
 
 

time: 20.5 us -> 17.2 us (0.84)
  Pallas kernels: 19.7 us -> 16.4 us
    pallas_call x1 -> x0, Pallas kernels: 3.34 us -> none  [on_device(): pl.pallas_call(store_kernel, out_shape=jax.ShapeDtypeStruct(out_shape, jn...]
    unnamed x2 -> x1, local copies, waits for them, and re-layouts: 0.61 us -> 0.64 us
where the time goes in v3:
time: 17.2 us; the launch traced here: 17 us
  Pallas kernels  16.4 us (95%)
  local copies, waits for them, and re-layouts  0.64 us (4%)
    pallas_call x1, Pallas kernels, on_device(): pl.pallas_call(functools.partial(kernel, sizes), out_shape=pltpu.VMEM(out...  16.4 us
    unnamed x1, local copies, waits for them, and re-layouts  0.64 us

profile of v3, /device:TPU:0, one launch (start us, length us, event | category | flops | bytes accessed | tf_op | source)
XLA Modules:
  0.0 17.0 jit_solution(17236830022856397735)
XLA Ops:
  0.0 16.4 %shard_map.73 = bf16[1,48,768]{2,1,0:T(8,128)(2,1)S(1)} custom-call(bf16[4,2,32,2048]{3,2,1,0:T(8,128)(2,1)} %vis_hbm.1, bf16[2,384,1024]{2,1,0:T(8,128)(2,1)} %constant.2.clone.table_hbm, bf16[4,32,768]{2,1,0:T(8,128)(2,1)} %beam_hbm.1, f32[48,768]{1,0:T(8,128)} %gain_hbm.1, bf16[768,768]{1,0:T(8,128)(2,1)} %basis_hbm.1, f32[4]{0:T(128)} %step_hbm.1, ...), custom_call_target="tpu_custom_call" | custom-call | tf_op jit(solution)/shard_map/pallas_call | solution.py:276
  16.4 0.6 %copy.9 = bf16[48,1,1,768]{3,0,2,1:T(8,128)(2,1)} copy(bf16[48,1,1,768]{3,0,2,1:T(8,128)(2,1)S(1)} %bitcast.1) | data formatting | bytes 147456

commit v4 on v3

--- a/solution.py
+++ b/solution.py
@@ -66,38 +66,47 @@
     half = nfreq * nbase
     full = n_pol * half
     kept = kl_v.shape[0] // n_freq
-    peers = [(da, dp) for da in range(n_ma) for dp in range(n_pol) if (da, dp) != (0, 0)]
-    peers.sort(key=lambda o: (abs(o[0] - n_ma // 2), o[1]))
-
-    tchunks = table_v.shape[0]
-    tsize = ntime // tchunks
-    spectral = []
+    pieces = 2 if n_ma % 2 == 0 else 1
+    span = n_ma // pieces
+    starts = [lax.rem(a // span + 1 + piece, pieces) * span for piece in range(pieces)]
+
+    tchunks, tsize = table_v.shape[0], table_v.shape[-1]
+    vis_loads, table_loads = [], [[] for _ in range(pieces)]
+
+    def load_table(piece, i):
+        part = pl.ds(starts[piece], span)
+        sem = load_sem.at[tchunks * (2 + piece) + i]
+        copy = pltpu.make_async_copy(table_hbm.at[i, part], table_v.at[i, part], sem)
+        copy.start()
+        table_loads[piece].append(copy)
+
     for i in range(tchunks):
         cols = pl.ds(i * tsize, tsize)
         group = [
             pltpu.make_async_copy(
-                vis_hbm.at[:, part, :, cols], vis_v.at[part, :, :, cols], load_sem.at[3 * i + part]
+                vis_hbm.at[:, part, :, cols], vis_v.at[part, :, :, cols], load_sem.at[2 * i + part]
             )
             for part in range(2)
         ]
-        group.append(pltpu.make_async_copy(table_hbm.at[i], table_v.at[i], load_sem.at[3 * i + 2]))
         for c in group:
             c.start()
-        spectral.append(group)
+        vis_loads.append(group)
+        load_table(0, i)
+    for piece in range(1, pieces):
+        for i in range(tchunks):
+            load_table(piece, i)
     loads = [
-        pltpu.make_async_copy(src, dst, load_sem.at[3 * tchunks + i])
+        pltpu.make_async_copy(src, dst, load_sem.at[tchunks * (2 + pieces) + i])
         for i, (src, dst) in enumerate(
             [
                 (step_hbm, step_s),
                 (kl_hbm, kl_v),
-                (basis_hbm, basis_v),
                 (beam_hbm, beam_v.at[fr, p]),
                 (gain_hbm, gain_v),
+                (basis_hbm, basis_v),
             ]
         )
     ]
-    for c in loads:
-        c.start()
 
     barrier = pltpu.get_barrier_semaphore()
 
@@ -119,39 +128,53 @@
         copy.start()
         return copy
 
-    for da, dp in peers:
+    for da, dp in [(da, dp) for da in range(n_ma) for dp in range(n_pol)][1:]:
         pl.semaphore_signal(barrier, inc=1, device_id=group_id(da, dp), device_id_type=MESH)
     for df in range(1, n_freq):
         pl.semaphore_signal(barrier, inc=1, device_id=freq_id(df), device_id_type=MESH)
 
-    total = None
-    for i in range(tchunks):
-        for c in spectral[i]:
-            c.wait()
-        samples = vis_v[:, :, :, i * tsize : (i + 1) * tsize].reshape(2 * half, tsize)
-        term = dot_t(table_v[i], samples)
-        total = term if total is None else total + term
-    cosine, sine = total[:all_modes], total[all_modes:]
-    real = cosine[:, :half] + sine[:, half:]
-    imag = cosine[:, half:] - sine[:, :half]
-    turn = lax.rem(a * lax.broadcasted_iota(jnp.int32, (all_modes, half), 0), n_ma)
     scale = float(ntime * n_ma) ** -0.5
-    pc = jnp.full((all_modes, half), scale, jnp.float32)
-    ps = jnp.zeros((all_modes, half), jnp.float32)
-    for r in range(1, n_ma):
-        angle = 2.0 * np.pi * r / n_ma
-        pc = jnp.where(turn == r, float(scale * np.cos(angle)), pc)
-        ps = jnp.where(turn == r, float(scale * np.sin(angle)), ps)
-    block = (n_ma, local_modes, half)
-    send_v[0] = (real * pc + imag * ps).astype(jnp.bfloat16).reshape(block)
-    send_v[1] = (imag * pc - real * ps).astype(jnp.bfloat16).reshape(block)
-
-    pl.semaphore_wait(barrier, len(peers) + n_freq - 1)
+    shape = (span, local_modes, half)
     copies = []
-    for i, (da, dp) in enumerate(peers):
-        to = group_id(da, dp)
-        src = send_v.at[to["pol"], to["ma"]]
-        copies.append(remote(src, recv_v.at[p, a], send_sem.at[i], recv_sem.at[i], to))
+    for piece, start in enumerate(starts):
+        total = None
+        for i in range(tchunks):
+            if piece == 0:
+                for c in vis_loads[i]:
+                    c.wait()
+            table_loads[piece][i].wait()
+            if piece == 0 and i == tchunks - 1:
+                for c in loads:
+                    c.start()
+            samples = vis_v[:, :, :, i * tsize : (i + 1) * tsize].reshape(2 * half, tsize)
+            term = dot_t(table_v[i, pl.ds(start, span)].reshape(-1, tsize), samples)
+            total = term if total is None else total + term
+        total = total.reshape(span, 2, local_modes, 2 * half)
+        real = total[:, 0, :, :half] + total[:, 1, :, half:]
+        imag = total[:, 0, :, half:] - total[:, 1, :, :half]
+        mode = lax.broadcasted_iota(jnp.int32, shape, 1) + local_modes * (
+            start + lax.broadcasted_iota(jnp.int32, shape, 0)
+        )
+        turn = lax.rem(a * mode, n_ma)
+        pc = jnp.full(shape, scale, jnp.float32)
+        ps = jnp.zeros(shape, jnp.float32)
+        for r in range(1, n_ma):
+            angle = 2.0 * np.pi * r / n_ma
+            pc = jnp.where(turn == r, float(scale * np.cos(angle)), pc)
+            ps = jnp.where(turn == r, float(scale * np.sin(angle)), ps)
+        send_v[0, pl.ds(start, span)] = (real * pc + imag * ps).astype(jnp.bfloat16)
+        send_v[1, pl.ds(start, span)] = (imag * pc - real * ps).astype(jnp.bfloat16)
+
+        if piece == 0:
+            pl.semaphore_wait(barrier, n_ma * n_pol - 1 + n_freq - 1)
+        for i in range(span):
+            for dp in range(n_pol):
+                if piece == pieces - 1 and (i, dp) == (0, 0):
+                    continue
+                to = {"ma": start + lax.rem(a + i, span), "pol": lax.rem(p + dp, n_pol)}
+                src = send_v.at[to["pol"], to["ma"]]
+                n = len(copies)
+                copies.append(remote(src, recv_v.at[p, a], send_sem.at[n], recv_sem.at[n], to))
     mine = beam_v.at[fr, p]
     pol_copies = [
         remote(beam_hbm, mine, pol_sem.at[0, d - 1], pol_sem.at[1, d - 1], group_id(0, d))
@@ -243,16 +266,16 @@
         for j in range(kept):
             ysend_v[d - 1, j] = (y * weights[d][j]).astype(jnp.bfloat16)
         sems = (y_sem.at[0, d - 1], y_sem.at[1, d - 1])
-        y_copies.append(remote(ysend_v.at[d - 1], yrecv_v.at[fr], *sems, freq_id(d)))
-    for j in range(kept):
-        yrecv_v[fr, j] = (y * weights[0][j]).astype(jnp.bfloat16)
-
+        y_copies.append(remote(ysend_v.at[d - 1], yrecv_v.at[d - 1], *sems, freq_id(d)))
+
+    left = jnp.concatenate([y * w for w in weights[0]], axis=0).astype(jnp.bfloat16)
+    g = dot(left, beam_v[fr].reshape(full, degrees))
     for copy in pass_copies + y_copies:
         copy.wait_recv()
-    left = jnp.concatenate(
-        [yrecv_v[s].reshape(kept * local_modes, full) for s in range(n_freq)], axis=1
-    )
-    g = dot(left, beam_v[...].reshape(n_freq * full, degrees))
+    for d in range(1, n_freq):
+        left = yrecv_v[d - 1].reshape(kept * local_modes, full)
+        source = lax.rem(fr + n_freq - d, n_freq)
+        g = g + dot(left, beam_v[source].reshape(full, degrees))
     out_ref[...] = masked(dot(with_gain(g), basis_v[...])).reshape(out_ref.shape)
     for copy in copies + pol_copies + freq_copies + pass_copies + y_copies:
         copy.wait_send()
@@ -268,7 +291,8 @@
     all_modes = local_modes * n_ma
     tchunks = 2 if ntime % 512 == 0 else 1
     table = spectral_tables(all_modes, ntime, ntime * n_ma)
-    table = np.ascontiguousarray(table.reshape(2 * all_modes, tchunks, -1).transpose(1, 0, 2))
+    table = table.reshape(2, n_ma, local_modes, tchunks, -1).transpose(3, 1, 0, 2, 4)
+    table = np.ascontiguousarray(table)
     peers = n_ma * n_pol - 1
     hops, cores = max(n_freq - 1, 1), max(n_pol - 1, 1)
     dma = pltpu.SemaphoreType.DMA
@@ -289,8 +313,8 @@
             pltpu.VMEM((2, n_ma, local_modes, half), jnp.bfloat16),
             pltpu.VMEM((n_pol, n_ma, local_modes, half), jnp.bfloat16),
             pltpu.VMEM((hops, kept, local_modes, full), jnp.bfloat16),
-            pltpu.VMEM((n_freq, kept, local_modes, full), jnp.bfloat16),
-            dma((3 * tchunks + 5,)),
+            pltpu.VMEM((hops, kept, local_modes, full), jnp.bfloat16),
+            dma((4 * tchunks + 5,)),
             dma((peers,)),
             dma((peers,)),
             dma((2, cores)),

time: 17.2 us -> 17.9 us (1.041)
  Pallas kernels: 16.4 us -> 17.1 us
    pallas_call x1, Pallas kernels: 16.4 us -> 17.1 us  [on_device(): pl.pallas_call(functools.partial(kernel, sizes), out_shape=pltpu.VMEM(out...]
where the time goes in v4:
time: 17.9 us; the launch traced here: 17.7 us
  Pallas kernels  17.1 us (96%)
  local copies, waits for them, and re-layouts  0.64 us (4%)
    pallas_call x1, Pallas kernels, on_device(): pl.pallas_call(functools.partial(kernel, sizes), out_shape=pltpu.VMEM(out...  17.1 us
    unnamed x1, local copies, waits for them, and re-layouts  0.64 us

profile of v4, /device:TPU:0, one launch (start us, length us, event | category | flops | bytes accessed | tf_op | source)
XLA Modules:
  0.0 17.7 jit_solution(18282238236447351178)
XLA Ops:
  0.0 17.1 %shard_map.73 = bf16[1,48,768]{2,1,0:T(8,128)(2,1)S(1)} custom-call(bf16[4,2,32,2048]{3,2,1,0:T(8,128)(2,1)} %vis_hbm.1, bf16[2,4,2,48,1024]{4,3,2,1,0:T(8,128)(2,1)} %constant.2.clone.table_hbm, bf16[4,32,768]{2,1,0:T(8,128)(2,1)} %beam_hbm.1, f32[48,768]{1,0:T(8,128)} %gain_hbm.1, bf16[768,768]{1,0:T(8,128)(2,1)} %basis_hbm.1, f32[4]{0:T(128)} %step_hbm.1, ...), custom_call_target="tpu_custom_call" | custom-call | tf_op jit(solution)/shard_map/pallas_call | solution.py:300
  17.1 0.6 %copy.9 = bf16[48,1,1,768]{3,0,2,1:T(8,128)(2,1)} copy(bf16[48,1,1,768]{3,0,2,1:T(8,128)(2,1)S(1)} %bitcast.1) | data formatting | bytes 147456

commit v5 on v3

--- a/solution.py
+++ b/solution.py
@@ -11,7 +11,6 @@
 
 ITERS = 2
 MESH = pl.DeviceIdType.MESH
-NT_DIMS = (((1,), (1,)), ((), ()))
 
 
 def spectral_tables(modes, local_time, total):
@@ -23,10 +22,6 @@
 
 def dot(left, right):
     return jnp.dot(left, right, preferred_element_type=jnp.float32)
-
-
-def dot_t(left, right):
-    return lax.dot_general(left, right, NT_DIMS, preferred_element_type=jnp.float32)
 
 
 def kernel(
@@ -44,6 +39,8 @@
     beam_v,
     gain_v,
     basis_v,
+    basis_t,
+    rows_t,
     step_s,
     kl_v,
     send_v,
@@ -129,8 +126,9 @@
         for c in spectral[i]:
             c.wait()
         samples = vis_v[:, :, :, i * tsize : (i + 1) * tsize].reshape(2 * half, tsize)
-        term = dot_t(table_v[i], samples)
+        term = dot(samples, table_v[i])
         total = term if total is None else total + term
+    total = total.T
     cosine, sine = total[:all_modes], total[all_modes:]
     real = cosine[:, :half] + sine[:, half:]
     imag = cosine[:, half:] - sine[:, :half]
@@ -192,7 +190,11 @@
     for f in range(nfreq):
         steps = jnp.where(own[f][:1], step_s[f], steps)
 
-    for copy in pol_copies + copies:
+    basis_t[...] = basis_v[...].T
+    for copy in pol_copies:
+        copy.wait_recv()
+    rows_t[...] = beam_v[fr].reshape(full, degrees).T
+    for copy in copies:
         copy.wait_recv()
 
     def spread(value):
@@ -217,7 +219,7 @@
     def again(y):
         rows = beam_v[fr].reshape(full, degrees)
         coeffs = masked(dot(with_gain(dot(spread(y), rows)), basis_v[...]))
-        return gather(dot_t(with_gain(dot_t(coeffs, basis_v[...])), rows))
+        return gather(dot(with_gain(dot(coeffs, basis_t[...])), rows_t[...]))
 
     halves = []
     for q in range(n_pol):
@@ -243,16 +245,16 @@
         for j in range(kept):
             ysend_v[d - 1, j] = (y * weights[d][j]).astype(jnp.bfloat16)
         sems = (y_sem.at[0, d - 1], y_sem.at[1, d - 1])
-        y_copies.append(remote(ysend_v.at[d - 1], yrecv_v.at[fr], *sems, freq_id(d)))
-    for j in range(kept):
-        yrecv_v[fr, j] = (y * weights[0][j]).astype(jnp.bfloat16)
-
+        y_copies.append(remote(ysend_v.at[d - 1], yrecv_v.at[d - 1], *sems, freq_id(d)))
+
+    left = jnp.concatenate([y * w for w in weights[0]], axis=0).astype(jnp.bfloat16)
+    g = dot(left, beam_v[fr].reshape(full, degrees))
     for copy in pass_copies + y_copies:
         copy.wait_recv()
-    left = jnp.concatenate(
-        [yrecv_v[s].reshape(kept * local_modes, full) for s in range(n_freq)], axis=1
-    )
-    g = dot(left, beam_v[...].reshape(n_freq * full, degrees))
+    for d in range(1, n_freq):
+        left = yrecv_v[d - 1].reshape(kept * local_modes, full)
+        source = lax.rem(fr + n_freq - d, n_freq)
+        g = g + dot(left, beam_v[source].reshape(full, degrees))
     out_ref[...] = masked(dot(with_gain(g), basis_v[...])).reshape(out_ref.shape)
     for copy in copies + pol_copies + freq_copies + pass_copies + y_copies:
         copy.wait_send()
@@ -268,7 +270,7 @@
     all_modes = local_modes * n_ma
     tchunks = 2 if ntime % 512 == 0 else 1
     table = spectral_tables(all_modes, ntime, ntime * n_ma)
-    table = np.ascontiguousarray(table.reshape(2 * all_modes, tchunks, -1).transpose(1, 0, 2))
+    table = np.ascontiguousarray(table.T).reshape(tchunks, -1, 2 * all_modes)
     peers = n_ma * n_pol - 1
     hops, cores = max(n_freq - 1, 1), max(n_pol - 1, 1)
     dma = pltpu.SemaphoreType.DMA
@@ -284,12 +286,14 @@
             pltpu.VMEM((n_freq, n_pol, nfreq, nbase, degrees), jnp.bfloat16),
             pltpu.VMEM((local_modes, degrees), jnp.float32),
             pltpu.VMEM(harmonic_basis.shape, jnp.bfloat16),
+            pltpu.VMEM(harmonic_basis.shape[::-1], jnp.bfloat16),
+            pltpu.VMEM((degrees, full), jnp.bfloat16),
             pltpu.SMEM(step_size.shape, jnp.float32),
             pltpu.VMEM(kl_matrix.shape, jnp.bfloat16),
             pltpu.VMEM((2, n_ma, local_modes, half), jnp.bfloat16),
             pltpu.VMEM((n_pol, n_ma, local_modes, half), jnp.bfloat16),
             pltpu.VMEM((hops, kept, local_modes, full), jnp.bfloat16),
-            pltpu.VMEM((n_freq, kept, local_modes, full), jnp.bfloat16),
+            pltpu.VMEM((hops, kept, local_modes, full), jnp.bfloat16),
             dma((3 * tchunks + 5,)),
             dma((peers,)),
             dma((peers,)),

time: 17.2 us -> 17 us (0.988)
  Pallas kernels: 16.4 us -> 16.2 us
    pallas_call x1, Pallas kernels: 16.4 us -> 16.2 us  [on_device(): pl.pallas_call(functools.partial(kernel, sizes), out_shape=pltpu.VMEM(out...]
where the time goes in v5:
time: 17 us; the launch traced here: 16.9 us
  Pallas kernels  16.2 us (95%)
  local copies, waits for them, and re-layouts  0.64 us (4%)
    pallas_call x1, Pallas kernels, on_device(): pl.pallas_call(functools.partial(kernel, sizes), out_shape=pltpu.VMEM(out...  16.2 us
    unnamed x1, local copies, waits for them, and re-layouts  0.64 us

profile of v5, /device:TPU:0, one launch (start us, length us, event | category | flops | bytes accessed | tf_op | source)
XLA Modules:
  0.0 16.9 jit_solution(10323093969184329583)
XLA Ops:
  0.0 16.2 %shard_map.73 = bf16[1,48,768]{2,1,0:T(8,128)(2,1)S(1)} custom-call(bf16[4,2,32,2048]{3,2,1,0:T(8,128)(2,1)} %vis_hbm.1, bf16[2,1024,384]{2,1,0:T(8,128)(2,1)} %constant.2.clone.table_hbm, bf16[4,32,768]{2,1,0:T(8,128)(2,1)} %beam_hbm.1, f32[48,768]{1,0:T(8,128)} %gain_hbm.1, bf16[768,768]{1,0:T(8,128)(2,1)} %basis_hbm.1, f32[4]{0:T(128)} %step_hbm.1, ...), custom_call_target="tpu_custom_call" | custom-call | tf_op jit(solution)/shard_map/pallas_call | solution.py:278
  16.2 0.6 %copy.9 = bf16[48,1,1,768]{3,0,2,1:T(8,128)(2,1)} copy(bf16[48,1,1,768]{3,0,2,1:T(8,128)(2,1)S(1)} %bitcast.1) | data formatting | bytes 147456

commit v6 on v5

--- a/solution.py
+++ b/solution.py
@@ -13,11 +13,12 @@
 MESH = pl.DeviceIdType.MESH
 
 
-def spectral_tables(modes, local_time, total):
-    phase = np.outer(np.arange(modes), np.arange(local_time)) % total
+def spectral_tables(modes, times, total):
+    phase = np.outer(np.arange(times), np.arange(modes)) % total
     angle = phase * (2.0 * np.pi / total)
-    both = np.concatenate([np.cos(angle), np.sin(angle)], axis=0)
-    return both.astype(np.float32).astype(ml_dtypes.bfloat16)
+    both = np.zeros((times, 2, -(-modes // 128) * 128), np.float32)
+    both[:, 0, :modes], both[:, 1, :modes] = np.cos(angle), np.sin(angle)
+    return both.reshape(times, -1).astype(ml_dtypes.bfloat16)
 
 
 def dot(left, right):
@@ -66,23 +67,25 @@
     peers = [(da, dp) for da in range(n_ma) for dp in range(n_pol) if (da, dp) != (0, 0)]
     peers.sort(key=lambda o: (abs(o[0] - n_ma // 2), o[1]))
 
-    tchunks = table_v.shape[0]
-    tsize = ntime // tchunks
-    spectral = []
+    tsize, lanes = table_v.shape[0], table_v.shape[1] // 2
+    tchunks = ntime // tsize
+    load_table = pltpu.make_async_copy(table_hbm, table_v, load_sem.at[2 * tchunks])
+    vis_loads = []
     for i in range(tchunks):
         cols = pl.ds(i * tsize, tsize)
         group = [
             pltpu.make_async_copy(
-                vis_hbm.at[:, part, :, cols], vis_v.at[part, :, :, cols], load_sem.at[3 * i + part]
+                vis_hbm.at[:, part, :, cols], vis_v.at[part, :, :, cols], load_sem.at[2 * i + part]
             )
             for part in range(2)
         ]
-        group.append(pltpu.make_async_copy(table_hbm.at[i], table_v.at[i], load_sem.at[3 * i + 2]))
         for c in group:
             c.start()
-        spectral.append(group)
+        if i == 0:
+            load_table.start()
+        vis_loads.append(group)
     loads = [
-        pltpu.make_async_copy(src, dst, load_sem.at[3 * tchunks + i])
+        pltpu.make_async_copy(src, dst, load_sem.at[2 * tchunks + 1 + i])
         for i, (src, dst) in enumerate(
             [
                 (step_hbm, step_s),
@@ -121,28 +124,31 @@
     for df in range(1, n_freq):
         pl.semaphore_signal(barrier, inc=1, device_id=freq_id(df), device_id_type=MESH)
 
-    total = None
+    scale = float(ntime * n_ma) ** -0.5
+    order = n_ma * tchunks
+    mode = lax.broadcasted_iota(jnp.int32, (1, lanes), 1)
+    real = imag = 0.0
     for i in range(tchunks):
-        for c in spectral[i]:
+        turn = lax.rem((a * tchunks + i) * mode, order)
+        pc = jnp.full((1, lanes), scale, jnp.float32)
+        ps = jnp.zeros((1, lanes), jnp.float32)
+        for r in range(1, order):
+            angle = 2.0 * np.pi * r / order
+            pc = jnp.where(turn == r, float(scale * np.cos(angle)), pc)
+            ps = jnp.where(turn == r, float(scale * np.sin(angle)), ps)
+        for c in vis_loads[i]:
             c.wait()
+        if i == 0:
+            load_table.wait()
         samples = vis_v[:, :, :, i * tsize : (i + 1) * tsize].reshape(2 * half, tsize)
-        term = dot(samples, table_v[i])
-        total = term if total is None else total + term
-    total = total.T
-    cosine, sine = total[:all_modes], total[all_modes:]
-    real = cosine[:, :half] + sine[:, half:]
-    imag = cosine[:, half:] - sine[:, :half]
-    turn = lax.rem(a * lax.broadcasted_iota(jnp.int32, (all_modes, half), 0), n_ma)
-    scale = float(ntime * n_ma) ** -0.5
-    pc = jnp.full((all_modes, half), scale, jnp.float32)
-    ps = jnp.zeros((all_modes, half), jnp.float32)
-    for r in range(1, n_ma):
-        angle = 2.0 * np.pi * r / n_ma
-        pc = jnp.where(turn == r, float(scale * np.cos(angle)), pc)
-        ps = jnp.where(turn == r, float(scale * np.sin(angle)), ps)
+        total = dot(samples, table_v[...])
+        first = total[:half, :lanes] + total[half:, lanes:]
+        second = total[half:, :lanes] - total[:half, lanes:]
+        real = real + (first * pc + second * ps)
+        imag = imag + (second * pc - first * ps)
     block = (n_ma, local_modes, half)
-    send_v[0] = (real * pc + imag * ps).astype(jnp.bfloat16).reshape(block)
-    send_v[1] = (imag * pc - real * ps).astype(jnp.bfloat16).reshape(block)
+    send_v[0] = real.T[:all_modes].astype(jnp.bfloat16).reshape(block)
+    send_v[1] = imag.T[:all_modes].astype(jnp.bfloat16).reshape(block)
 
     pl.semaphore_wait(barrier, len(peers) + n_freq - 1)
     copies = []
@@ -268,9 +274,8 @@
     half = nfreq * nbase
     full = n_pol * half
     all_modes = local_modes * n_ma
-    tchunks = 2 if ntime % 512 == 0 else 1
-    table = spectral_tables(all_modes, ntime, ntime * n_ma)
-    table = np.ascontiguousarray(table.T).reshape(tchunks, -1, 2 * all_modes)
+    tchunks = 4 if ntime % 1024 == 0 else 1
+    table = spectral_tables(all_modes, ntime // tchunks, ntime * n_ma)
     peers = n_ma * n_pol - 1
     hops, cores = max(n_freq - 1, 1), max(n_pol - 1, 1)
     dma = pltpu.SemaphoreType.DMA
@@ -294,7 +299,7 @@
             pltpu.VMEM((n_pol, n_ma, local_modes, half), jnp.bfloat16),
             pltpu.VMEM((hops, kept, local_modes, full), jnp.bfloat16),
             pltpu.VMEM((hops, kept, local_modes, full), jnp.bfloat16),
-            dma((3 * tchunks + 5,)),
+            dma((2 * tchunks + 6,)),
             dma((peers,)),
             dma((peers,)),
             dma((2, cores)),

time: 17 us -> 17 us (level)
  no operation moved by 1% of the time
where the time goes in v6:
time: 17 us; the launch traced here: 16.9 us
  Pallas kernels  16.2 us (95%)
  local copies, waits for them, and re-layouts  0.64 us (4%)
    pallas_call x1, Pallas kernels, on_device(): pl.pallas_call(functools.partial(kernel, sizes), out_shape=pltpu.VMEM(out...  16.2 us
    unnamed x1, local copies, waits for them, and re-layouts  0.64 us

profile of v6, /device:TPU:0, one launch (start us, length us, event | category | flops | bytes accessed | tf_op | source)
XLA Modules:
  0.0 16.9 jit_solution(14516504165948439541)
XLA Ops:
  0.0 16.2 %shard_map.73 = bf16[1,48,768]{2,1,0:T(8,128)(2,1)S(1)} custom-call(bf16[4,2,32,2048]{3,2,1,0:T(8,128)(2,1)} %vis_hbm.1, bf16[512,512]{1,0:T(8,128)(2,1)} %constant.2.clone.table_hbm, bf16[4,32,768]{2,1,0:T(8,128)(2,1)} %beam_hbm.1, f32[48,768]{1,0:T(8,128)} %gain_hbm.1, bf16[768,768]{1,0:T(8,128)(2,1)} %basis_hbm.1, f32[4]{0:T(128)} %step_hbm.1, ...), custom_call_target="tpu_custom_call" | custom-call | tf_op jit(solution)/shard_map/pallas_call | solution.py:283
  16.3 0.6 %copy.9 = bf16[48,1,1,768]{3,0,2,1:T(8,128)(2,1)} copy(bf16[48,1,1,768]{3,0,2,1:T(8,128)(2,1)S(1)} %bitcast.1) | data formatting | bytes 147456

commit v7 on v5

--- a/solution.py
+++ b/solution.py
@@ -66,6 +66,31 @@
     peers = [(da, dp) for da in range(n_ma) for dp in range(n_pol) if (da, dp) != (0, 0)]
     peers.sort(key=lambda o: (abs(o[0] - n_ma // 2), o[1]))
 
+    barrier = pltpu.get_barrier_semaphore()
+
+    def group_id(da, dp):
+        return {"ma": lax.rem(a + da, n_ma), "pol": lax.rem(p + dp, n_pol)}
+
+    def freq_id(df):
+        return {"freq": lax.rem(fr + df, n_freq)}
+
+    def remote(src, dst, send, recv, to):
+        copy = pltpu.make_async_remote_copy(
+            src_ref=src,
+            dst_ref=dst,
+            send_sem=send,
+            recv_sem=recv,
+            device_id=to,
+            device_id_type=MESH,
+        )
+        copy.start()
+        return copy
+
+    for da, dp in peers:
+        pl.semaphore_signal(barrier, inc=1, device_id=group_id(da, dp), device_id_type=MESH)
+    for df in range(1, n_freq):
+        pl.semaphore_signal(barrier, inc=1, device_id=freq_id(df), device_id_type=MESH)
+
     tchunks = table_v.shape[0]
     tsize = ntime // tchunks
     spectral = []
@@ -96,31 +121,6 @@
     for c in loads:
         c.start()
 
-    barrier = pltpu.get_barrier_semaphore()
-
-    def group_id(da, dp):
-        return {"ma": lax.rem(a + da, n_ma), "pol": lax.rem(p + dp, n_pol)}
-
-    def freq_id(df):
-        return {"freq": lax.rem(fr + df, n_freq)}
-
-    def remote(src, dst, send, recv, to):
-        copy = pltpu.make_async_remote_copy(
-            src_ref=src,
-            dst_ref=dst,
-            send_sem=send,
-            recv_sem=recv,
-            device_id=to,
-            device_id_type=MESH,
-        )
-        copy.start()
-        return copy
-
-    for da, dp in peers:
-        pl.semaphore_signal(barrier, inc=1, device_id=group_id(da, dp), device_id_type=MESH)
-    for df in range(1, n_freq):
-        pl.semaphore_signal(barrier, inc=1, device_id=freq_id(df), device_id_type=MESH)
-
     total = None
     for i in range(tchunks):
         for c in spectral[i]:
@@ -128,6 +128,17 @@
         samples = vis_v[:, :, :, i * tsize : (i + 1) * tsize].reshape(2 * half, tsize)
         term = dot(samples, table_v[i])
         total = term if total is None else total + term
+        if i == 0:
+            pl.semaphore_wait(barrier, len(peers) + n_freq - 1)
+            mine = beam_v.at[fr, p]
+            pol_copies = [
+                remote(beam_hbm, mine, pol_sem.at[0, d - 1], pol_sem.at[1, d - 1], group_id(0, d))
+                for d in range(1, n_pol)
+            ]
+            freq_copies = [
+                remote(beam_hbm, mine, freq_sem.at[0, d - 1], freq_sem.at[1, d - 1], freq_id(d))
+                for d in range(1, n_freq)
+            ]
     total = total.T
     cosine, sine = total[:all_modes], total[all_modes:]
     real = cosine[:, :half] + sine[:, half:]
@@ -144,21 +155,11 @@
     send_v[0] = (real * pc + imag * ps).astype(jnp.bfloat16).reshape(block)
     send_v[1] = (imag * pc - real * ps).astype(jnp.bfloat16).reshape(block)
 
-    pl.semaphore_wait(barrier, len(peers) + n_freq - 1)
     copies = []
     for i, (da, dp) in enumerate(peers):
         to = group_id(da, dp)
         src = send_v.at[to["pol"], to["ma"]]
         copies.append(remote(src, recv_v.at[p, a], send_sem.at[i], recv_sem.at[i], to))
-    mine = beam_v.at[fr, p]
-    pol_copies = [
-        remote(beam_hbm, mine, pol_sem.at[0, d - 1], pol_sem.at[1, d - 1], group_id(0, d))
-        for d in range(1, n_pol)
-    ]
-    freq_copies = [
-        remote(beam_hbm, mine, freq_sem.at[0, d - 1], freq_sem.at[1, d - 1], freq_id(d))
-        for d in range(1, n_freq)
-    ]
     recv_v[p, a] = send_v[p, a]
 
     for c in loads:

time: 17 us -> 17 us (level)
  no operation moved by 1% of the time
where the time goes in v7:
time: 17 us; the launch traced here: 16.8 us
  Pallas kernels  16.2 us (95%)
  local copies, waits for them, and re-layouts  0.64 us (4%)
    pallas_call x1, Pallas kernels, on_device(): pl.pallas_call(functools.partial(kernel, sizes), out_shape=pltpu.VMEM(out...  16.2 us
    unnamed x1, local copies, waits for them, and re-layouts  0.64 us

profile of v7, /device:TPU:0, one launch (start us, length us, event | category | flops | bytes accessed | tf_op | source)
XLA Modules:
  0.0 16.8 jit_solution(9614297314298112392)
XLA Ops:
  0.0 16.2 %shard_map.73 = bf16[1,48,768]{2,1,0:T(8,128)(2,1)S(1)} custom-call(bf16[4,2,32,2048]{3,2,1,0:T(8,128)(2,1)} %vis_hbm.1, bf16[2,1024,384]{2,1,0:T(8,128)(2,1)} %constant.2.clone.table_hbm, bf16[4,32,768]{2,1,0:T(8,128)(2,1)} %beam_hbm.1, f32[48,768]{1,0:T(8,128)} %gain_hbm.1, bf16[768,768]{1,0:T(8,128)(2,1)} %basis_hbm.1, f32[4]{0:T(128)} %step_hbm.1, ...), custom_call_target="tpu_custom_call" | custom-call | tf_op jit(solution)/shard_map/pallas_call | solution.py:279
  16.2 0.6 %copy.9 = bf16[48,1,1,768]{3,0,2,1:T(8,128)(2,1)} copy(bf16[48,1,1,768]{3,0,2,1:T(8,128)(2,1)S(1)} %bitcast.1) | data formatting | bytes 147456

commit v8 on v4

--- a/solution.py
+++ b/solution.py
@@ -11,7 +11,6 @@
 
 ITERS = 2
 MESH = pl.DeviceIdType.MESH
-NT_DIMS = (((1,), (1,)), ((), ()))
 
 
 def spectral_tables(modes, local_time, total):
@@ -23,10 +22,6 @@
 
 def dot(left, right):
     return jnp.dot(left, right, preferred_element_type=jnp.float32)
-
-
-def dot_t(left, right):
-    return lax.dot_general(left, right, NT_DIMS, preferred_element_type=jnp.float32)
 
 
 def kernel(
@@ -44,6 +39,8 @@
     beam_v,
     gain_v,
     basis_v,
+    basis_t,
+    rows_t,
     step_s,
     kl_v,
     send_v,
@@ -66,15 +63,40 @@
     half = nfreq * nbase
     full = n_pol * half
     kept = kl_v.shape[0] // n_freq
-    pieces = 2 if n_ma % 2 == 0 else 1
+    pieces = table_v.shape[1]
     span = n_ma // pieces
-    starts = [lax.rem(a // span + 1 + piece, pieces) * span for piece in range(pieces)]
-
-    tchunks, tsize = table_v.shape[0], table_v.shape[-1]
+    halves_of_ma = [lax.rem(a // span + 1 + piece, pieces) for piece in range(pieces)]
+
+    barrier = pltpu.get_barrier_semaphore()
+
+    def group_id(da, dp):
+        return {"ma": lax.rem(a + da, n_ma), "pol": lax.rem(p + dp, n_pol)}
+
+    def freq_id(df):
+        return {"freq": lax.rem(fr + df, n_freq)}
+
+    def remote(src, dst, send, recv, to):
+        copy = pltpu.make_async_remote_copy(
+            src_ref=src,
+            dst_ref=dst,
+            send_sem=send,
+            recv_sem=recv,
+            device_id=to,
+            device_id_type=MESH,
+        )
+        copy.start()
+        return copy
+
+    for da, dp in [(da, dp) for da in range(n_ma) for dp in range(n_pol)][1:]:
+        pl.semaphore_signal(barrier, inc=1, device_id=group_id(da, dp), device_id_type=MESH)
+    for df in range(1, n_freq):
+        pl.semaphore_signal(barrier, inc=1, device_id=freq_id(df), device_id_type=MESH)
+
+    tchunks, tsize = table_v.shape[0], table_v.shape[2]
     vis_loads, table_loads = [], [[] for _ in range(pieces)]
 
     def load_table(piece, i):
-        part = pl.ds(starts[piece], span)
+        part = halves_of_ma[piece]
         sem = load_sem.at[tchunks * (2 + piece) + i]
         copy = pltpu.make_async_copy(table_hbm.at[i, part], table_v.at[i, part], sem)
         copy.start()
@@ -101,55 +123,41 @@
             [
                 (step_hbm, step_s),
                 (kl_hbm, kl_v),
+                (basis_hbm, basis_v),
                 (beam_hbm, beam_v.at[fr, p]),
                 (gain_hbm, gain_v),
-                (basis_hbm, basis_v),
             ]
         )
     ]
-
-    barrier = pltpu.get_barrier_semaphore()
-
-    def group_id(da, dp):
-        return {"ma": lax.rem(a + da, n_ma), "pol": lax.rem(p + dp, n_pol)}
-
-    def freq_id(df):
-        return {"freq": lax.rem(fr + df, n_freq)}
-
-    def remote(src, dst, send, recv, to):
-        copy = pltpu.make_async_remote_copy(
-            src_ref=src,
-            dst_ref=dst,
-            send_sem=send,
-            recv_sem=recv,
-            device_id=to,
-            device_id_type=MESH,
-        )
-        copy.start()
-        return copy
-
-    for da, dp in [(da, dp) for da in range(n_ma) for dp in range(n_pol)][1:]:
-        pl.semaphore_signal(barrier, inc=1, device_id=group_id(da, dp), device_id_type=MESH)
-    for df in range(1, n_freq):
-        pl.semaphore_signal(barrier, inc=1, device_id=freq_id(df), device_id_type=MESH)
+    for c in loads:
+        c.start()
 
     scale = float(ntime * n_ma) ** -0.5
     shape = (span, local_modes, half)
     copies = []
-    for piece, start in enumerate(starts):
+    for piece, part in enumerate(halves_of_ma):
+        start = part * span
         total = None
         for i in range(tchunks):
             if piece == 0:
                 for c in vis_loads[i]:
                     c.wait()
             table_loads[piece][i].wait()
-            if piece == 0 and i == tchunks - 1:
-                for c in loads:
-                    c.start()
             samples = vis_v[:, :, :, i * tsize : (i + 1) * tsize].reshape(2 * half, tsize)
-            term = dot_t(table_v[i, pl.ds(start, span)].reshape(-1, tsize), samples)
+            term = dot(samples, table_v[i, part])
             total = term if total is None else total + term
-        total = total.reshape(span, 2, local_modes, 2 * half)
+            if piece == 0 and i == 0:
+                pl.semaphore_wait(barrier, n_ma * n_pol - 1 + n_freq - 1)
+                mine = beam_v.at[fr, p]
+                pol_copies = [
+                    remote(beam_hbm, mine, pol_sem.at[0, d - 1], pol_sem.at[1, d - 1], group_id(0, d))
+                    for d in range(1, n_pol)
+                ]
+                freq_copies = [
+                    remote(beam_hbm, mine, freq_sem.at[0, d - 1], freq_sem.at[1, d - 1], freq_id(d))
+                    for d in range(1, n_freq)
+                ]
+        total = total.T.reshape(span, 2, local_modes, 2 * half)
         real = total[:, 0, :, :half] + total[:, 1, :, half:]
         imag = total[:, 0, :, half:] - total[:, 1, :, :half]
         mode = lax.broadcasted_iota(jnp.int32, shape, 1) + local_modes * (
@@ -165,8 +173,6 @@
         send_v[0, pl.ds(start, span)] = (real * pc + imag * ps).astype(jnp.bfloat16)
         send_v[1, pl.ds(start, span)] = (imag * pc - real * ps).astype(jnp.bfloat16)
 
-        if piece == 0:
-            pl.semaphore_wait(barrier, n_ma * n_pol - 1 + n_freq - 1)
         for i in range(span):
             for dp in range(n_pol):
                 if piece == pieces - 1 and (i, dp) == (0, 0):
@@ -175,15 +181,6 @@
                 src = send_v.at[to["pol"], to["ma"]]
                 n = len(copies)
                 copies.append(remote(src, recv_v.at[p, a], send_sem.at[n], recv_sem.at[n], to))
-    mine = beam_v.at[fr, p]
-    pol_copies = [
-        remote(beam_hbm, mine, pol_sem.at[0, d - 1], pol_sem.at[1, d - 1], group_id(0, d))
-        for d in range(1, n_pol)
-    ]
-    freq_copies = [
-        remote(beam_hbm, mine, freq_sem.at[0, d - 1], freq_sem.at[1, d - 1], freq_id(d))
-        for d in range(1, n_freq)
-    ]
     recv_v[p, a] = send_v[p, a]
 
     for c in loads:
@@ -215,7 +212,11 @@
     for f in range(nfreq):
         steps = jnp.where(own[f][:1], step_s[f], steps)
 
-    for copy in pol_copies + copies:
+    basis_t[...] = basis_v[...].T
+    for copy in pol_copies:
+        copy.wait_recv()
+    rows_t[...] = beam_v[fr].reshape(full, degrees).T
+    for copy in copies:
         copy.wait_recv()
 
     def spread(value):
@@ -240,7 +241,7 @@
     def again(y):
         rows = beam_v[fr].reshape(full, degrees)
         coeffs = masked(dot(with_gain(dot(spread(y), rows)), basis_v[...]))
-        return gather(dot_t(with_gain(dot_t(coeffs, basis_v[...])), rows))
+        return gather(dot(with_gain(dot(coeffs, basis_t[...])), rows_t[...]))
 
     halves = []
     for q in range(n_pol):
@@ -290,9 +291,12 @@
     full = n_pol * half
     all_modes = local_modes * n_ma
     tchunks = 2 if ntime % 512 == 0 else 1
+    pieces = 2 if n_ma % 2 == 0 else 1
     table = spectral_tables(all_modes, ntime, ntime * n_ma)
-    table = table.reshape(2, n_ma, local_modes, tchunks, -1).transpose(3, 1, 0, 2, 4)
-    table = np.ascontiguousarray(table)
+    table = table.reshape(2, pieces, n_ma // pieces, local_modes, tchunks, -1)
+    table = np.ascontiguousarray(table.transpose(4, 1, 5, 2, 0, 3)).reshape(
+        tchunks, pieces, ntime // tchunks, -1
+    )
     peers = n_ma * n_pol - 1
     hops, cores = max(n_freq - 1, 1), max(n_pol - 1, 1)
     dma = pltpu.SemaphoreType.DMA
@@ -308,13 +312,15 @@
             pltpu.VMEM((n_freq, n_pol, nfreq, nbase, degrees), jnp.bfloat16),
             pltpu.VMEM((local_modes, degrees), jnp.float32),
             pltpu.VMEM(harmonic_basis.shape, jnp.bfloat16),
+            pltpu.VMEM(harmonic_basis.shape[::-1], jnp.bfloat16),
+            pltpu.VMEM((degrees, full), jnp.bfloat16),
             pltpu.SMEM(step_size.shape, jnp.float32),
             pltpu.VMEM(kl_matrix.shape, jnp.bfloat16),
             pltpu.VMEM((2, n_ma, local_modes, half), jnp.bfloat16),
             pltpu.VMEM((n_pol, n_ma, local_modes, half), jnp.bfloat16),
             pltpu.VMEM((hops, kept, local_modes, full), jnp.bfloat16),
             pltpu.VMEM((hops, kept, local_modes, full), jnp.bfloat16),
-            dma((4 * tchunks + 5,)),
+            dma((tchunks * (2 + pieces) + 5,)),
             dma((peers,)),
             dma((peers,)),
             dma((2, cores)),

time: 17.9 us -> 17 us (0.950)
  Pallas kernels: 17.1 us -> 16.2 us
    pallas_call x1, Pallas kernels: 17.1 us -> 16.2 us  [on_device(): pl.pallas_call(functools.partial(kernel, sizes), out_shape=pltpu.VMEM(out...]
where the time goes in v8:
time: 17 us; the launch traced here: 16.8 us
  Pallas kernels  16.2 us (95%)
  local copies, waits for them, and re-layouts  0.64 us (4%)
    pallas_call x1, Pallas kernels, on_device(): pl.pallas_call(functools.partial(kernel, sizes), out_shape=pltpu.VMEM(out...  16.2 us
    unnamed x1, local copies, waits for them, and re-layouts  0.64 us

profile of v8, /device:TPU:0, one launch (start us, length us, event | category | flops | bytes accessed | tf_op | source)
XLA Modules:
  0.0 16.8 jit_solution(16109554806308626082)
XLA Ops:
  0.0 16.2 %shard_map.73 = bf16[1,48,768]{2,1,0:T(8,128)(2,1)S(1)} custom-call(bf16[4,2,32,2048]{3,2,1,0:T(8,128)(2,1)} %vis_hbm.1, bf16[2,2,1024,192]{3,2,1,0:T(8,128)(2,1)} %constant.2.clone.table_hbm, bf16[4,32,768]{2,1,0:T(8,128)(2,1)} %beam_hbm.1, f32[48,768]{1,0:T(8,128)} %gain_hbm.1, bf16[768,768]{1,0:T(8,128)(2,1)} %basis_hbm.1, f32[4]{0:T(128)} %step_hbm.1, ...), custom_call_target="tpu_custom_call" | custom-call | tf_op jit(solution)/shard_map/pallas_call | solution.py:304
  16.2 0.6 %copy.9 = bf16[48,1,1,768]{3,0,2,1:T(8,128)(2,1)} copy(bf16[48,1,1,768]{3,0,2,1:T(8,128)(2,1)S(1)} %bitcast.1) | data formatting | bytes 147456

commit v9 on v8

--- a/solution.py
+++ b/solution.py
@@ -22,6 +22,11 @@
 
 def dot(left, right):
     return jnp.dot(left, right, preferred_element_type=jnp.float32)
+
+
+def dot_t(left, right):
+    last = (((1,), (1,)), ((), ()))
+    return lax.dot_general(left, right, last, preferred_element_type=jnp.float32)
 
 
 def kernel(
@@ -39,8 +44,6 @@
     beam_v,
     gain_v,
     basis_v,
-    basis_t,
-    rows_t,
     step_s,
     kl_v,
     send_v,
@@ -212,11 +215,7 @@
     for f in range(nfreq):
         steps = jnp.where(own[f][:1], step_s[f], steps)
 
-    basis_t[...] = basis_v[...].T
-    for copy in pol_copies:
-        copy.wait_recv()
-    rows_t[...] = beam_v[fr].reshape(full, degrees).T
-    for copy in copies:
+    for copy in pol_copies + copies:
         copy.wait_recv()
 
     def spread(value):
@@ -241,7 +240,7 @@
     def again(y):
         rows = beam_v[fr].reshape(full, degrees)
         coeffs = masked(dot(with_gain(dot(spread(y), rows)), basis_v[...]))
-        return gather(dot(with_gain(dot(coeffs, basis_t[...])), rows_t[...]))
+        return gather(dot_t(with_gain(dot_t(coeffs, basis_v[...])), rows))
 
     halves = []
     for q in range(n_pol):
@@ -312,8 +311,6 @@
             pltpu.VMEM((n_freq, n_pol, nfreq, nbase, degrees), jnp.bfloat16),
             pltpu.VMEM((local_modes, degrees), jnp.float32),
             pltpu.VMEM(harmonic_basis.shape, jnp.bfloat16),
-            pltpu.VMEM(harmonic_basis.shape[::-1], jnp.bfloat16),
-            pltpu.VMEM((degrees, full), jnp.bfloat16),
             pltpu.SMEM(step_size.shape, jnp.float32),
             pltpu.VMEM(kl_matrix.shape, jnp.bfloat16),
             pltpu.VMEM((2, n_ma, local_modes, half), jnp.bfloat16),

time: 17 us -> 17 us (level)
  no operation moved by 1% of the time
where the time goes in v9:
time: 17 us; the launch traced here: 16.9 us
  Pallas kernels  16.2 us (95%)
  local copies, waits for them, and re-layouts  0.64 us (4%)
    pallas_call x1, Pallas kernels, on_device(): pl.pallas_call(functools.partial(kernel, sizes), out_shape=pltpu.VMEM(out...  16.2 us
    unnamed x1, local copies, waits for them, and re-layouts  0.64 us

profile of v9, /device:TPU:0, one launch (start us, length us, event | category | flops | bytes accessed | tf_op | source)
XLA Modules:
  0.0 16.9 jit_solution(9062842547164162722)
XLA Ops:
  0.0 16.2 %shard_map.73 = bf16[1,48,768]{2,1,0:T(8,128)(2,1)S(1)} custom-call(bf16[4,2,32,2048]{3,2,1,0:T(8,128)(2,1)} %vis_hbm.1, bf16[2,2,1024,192]{3,2,1,0:T(8,128)(2,1)} %constant.2.clone.table_hbm, bf16[4,32,768]{2,1,0:T(8,128)(2,1)} %beam_hbm.1, f32[48,768]{1,0:T(8,128)} %gain_hbm.1, bf16[768,768]{1,0:T(8,128)(2,1)} %basis_hbm.1, f32[4]{0:T(128)} %step_hbm.1, ...), custom_call_target="tpu_custom_call" | custom-call | tf_op jit(solution)/shard_map/pallas_call | solution.py:303
  16.3 0.6 %copy.9 = bf16[48,1,1,768]{3,0,2,1:T(8,128)(2,1)} copy(bf16[48,1,1,768]{3,0,2,1:T(8,128)(2,1)S(1)} %bitcast.1) | data formatting | bytes 147456

commit v10 on v7

--- a/solution.py
+++ b/solution.py
@@ -198,17 +198,6 @@
     for copy in copies:
         copy.wait_recv()
 
-    def spread(value):
-        return jnp.concatenate(
-            [jnp.where(own[f], value, 0.0) for f in range(nfreq)], axis=0
-        ).astype(jnp.bfloat16)
-
-    def gather(value):
-        result = jnp.zeros((local_modes, full), jnp.float32)
-        for f in range(nfreq):
-            result = jnp.where(own[f], value[f * local_modes : (f + 1) * local_modes], result)
-        return result
-
     def with_gain(value):
         value = value.reshape(-1, local_modes, degrees) * gain_v[...][None]
         return value.astype(jnp.bfloat16).reshape(-1, degrees)
@@ -217,10 +206,24 @@
         value = value.reshape(-1, local_modes, degrees)
         return jnp.where(keep[None], value, 0.0).astype(jnp.bfloat16).reshape(-1, degrees)
 
+    cut = (nfreq + 1) // 2
+    chains = [fs for fs in (range(cut), range(cut, nfreq)) if len(fs) > 0]
+
     def again(y):
         rows = beam_v[fr].reshape(full, degrees)
-        coeffs = masked(dot(with_gain(dot(spread(y), rows)), basis_v[...]))
-        return gather(dot(with_gain(dot(coeffs, basis_t[...])), rows_t[...]))
+        parts = [
+            jnp.concatenate([jnp.where(own[f], y, 0.0) for f in fs], axis=0).astype(jnp.bfloat16)
+            for fs in chains
+        ]
+        parts = [with_gain(dot(part, rows)) for part in parts]
+        parts = [masked(dot(part, basis_v[...])) for part in parts]
+        parts = [with_gain(dot(part, basis_t[...])) for part in parts]
+        parts = [dot(part, rows_t[...]) for part in parts]
+        result = jnp.zeros((local_modes, full), jnp.float32)
+        for fs, part in zip(chains, parts):
+            for i, f in enumerate(fs):
+                result = jnp.where(own[f], part[i * local_modes : (i + 1) * local_modes], result)
+        return result
 
     halves = []
     for q in range(n_pol):

time: 17 us -> 17.2 us (1.012)
  Pallas kernels: 16.2 us -> 16.4 us
    pallas_call x1, Pallas kernels: 16.2 us -> 16.4 us  [on_device(): pl.pallas_call(functools.partial(kernel, sizes), out_shape=pltpu.VMEM(out...]
where the time goes in v10:
time: 17.2 us; the launch traced here: 17 us
  Pallas kernels  16.4 us (95%)
  local copies, waits for them, and re-layouts  0.64 us (4%)
    pallas_call x1, Pallas kernels, on_device(): pl.pallas_call(functools.partial(kernel, sizes), out_shape=pltpu.VMEM(out...  16.4 us
    unnamed x1, local copies, waits for them, and re-layouts  0.64 us

profile of v10, /device:TPU:0, one launch (start us, length us, event | category | flops | bytes accessed | tf_op | source)
XLA Modules:
  0.0 17.0 jit_solution(986335831782895152)
XLA Ops:
  0.0 16.4 %shard_map.73 = bf16[1,48,768]{2,1,0:T(8,128)(2,1)S(1)} custom-call(bf16[4,2,32,2048]{3,2,1,0:T(8,128)(2,1)} %vis_hbm.1, bf16[2,1024,384]{2,1,0:T(8,128)(2,1)} %constant.2.clone.table_hbm, bf16[4,32,768]{2,1,0:T(8,128)(2,1)} %beam_hbm.1, f32[48,768]{1,0:T(8,128)} %gain_hbm.1, bf16[768,768]{1,0:T(8,128)(2,1)} %basis_hbm.1, f32[4]{0:T(128)} %step_hbm.1, ...), custom_call_target="tpu_custom_call" | custom-call | tf_op jit(solution)/shard_map/pallas_call | solution.py:282
  16.4 0.6 %copy.9 = bf16[48,1,1,768]{3,0,2,1:T(8,128)(2,1)} copy(bf16[48,1,1,768]{3,0,2,1:T(8,128)(2,1)S(1)} %bitcast.1) | data formatting | bytes 147456
